TPU v7x, 512 devices: a whole 4x4x16 slice. The times are simulated.
512 devices in a mesh: dp: 32 (over z, core), seq: 16 (over y, x).
Axes of the slice: x: 4, y: 4, z: 16, core: 2. Of those that a mesh axis runs over, the one named last changes fastest.
Arguments:
- query_input: bfloat16 [32, 16, 240, 1536], P('dp', 'seq'), may hold values from -8 to 8
- key_input: bfloat16 [32, 16, 240, 1536], P('dp', 'seq'), may hold values from -8 to 8
- value_input: bfloat16 [32, 16, 240, 1536], P('dp', 'seq'), may hold values from -6 to 6
- cotangent: bfloat16 [32, 16, 240, 1536], P('dp', 'seq'), may hold values from -6 to 6
- q_gain: float32 [1536], P('dp'), may hold values from 0.5 to 4
- k_gain: float32 [1536], P('dp'), may hold values from 0.5 to 4
- frames: int32 [32], P('dp'), may hold values from 8 to 16, as said below
- heights: int32 [32], P('dp'), may hold values from 7 to 15, as said below
- widths: int32 [32], P('dp'), may hold values from 8 to 16, as said below
Outputs:
- query_grad: bfloat16 [32, 16, 240, 1536], P('dp', 'seq')
- key_grad: bfloat16 [32, 16, 240, 1536], P('dp', 'seq')
- value_grad: bfloat16 [32, 16, 240, 1536], P('dp', 'seq')
- q_gain_grad: float32 [1536], P('dp')
- k_gain_grad: float32 [1536], P('dp')
Inputs may be any that keep to these rules, and one draw needn't show every extreme that they name: `frames`: at least half of 16 (and 1); some clip has all 16. `heights`: at least half of 15 (and 1); some clip has all 15. `widths`: at least half of 16 (and 1); some clip has all 16.
All inputs are finite; a program needn't handle non-finite values.
Results may differ from a plain program's by a relative error of at most 0.003.
The roundings to bfloat16 on the way count: a program that leaves them out, or rounds other values in their place, can miss the bound.
Values may be sent and summed in bfloat16 or wider, within the bound.
A program may use at most 64 MiB of HBM per device.

v0:
```python
import math

import jax
import jax.numpy as jnp
from jax import lax
from jax.sharding import PartitionSpec as P

HEAD_DIM = 128
PATCH_COLS = 16


EPS = 1e-06
NEGATIVE = -1e30


def normalize(inputs, gain, heads):
    values = inputs.astype(jnp.float32).reshape(inputs.shape[0], inputs.shape[1], heads, HEAD_DIM)
    inverse = lax.rsqrt(jnp.mean(values * values, axis=-1, keepdims=True) + EPS)
    scales = gain.reshape(heads, HEAD_DIM)
    return ((values * inverse * scales).astype(jnp.bfloat16), values, inverse, scales)


def attend(queries, keys, values, cotan, valid, seq_first):
    if seq_first:
        score_form, out_form, back_form = ("ibhd,jbhd->bhij", "bhij,jbhd->ibhd", "bhij,ibhd->jbhd")
        key_mask = jnp.transpose(valid)[:, None, None, :]
    else:
        score_form, out_form, back_form = ("bihd,bjhd->bhij", "bhij,bjhd->bihd", "bhij,bihd->bjhd")
        key_mask = valid[:, None, None, :]
    scale = 1.0 / math.sqrt(HEAD_DIM)
    f32 = jnp.float32
    scores = jnp.einsum(score_form, queries, keys, preferred_element_type=f32) * scale
    scores = jnp.where(key_mask, scores, NEGATIVE)
    top = jnp.max(scores, axis=-1, keepdims=True)
    expo = jnp.exp(scores - top)
    probs = expo / jnp.sum(expo, axis=-1, keepdims=True)
    probs_b = probs.astype(jnp.bfloat16)
    dprobs = jnp.einsum(score_form, cotan, values, preferred_element_type=f32)
    value_part = jnp.einsum(back_form, probs_b, cotan, preferred_element_type=f32)
    delta = jnp.sum(probs * dprobs, axis=-1, keepdims=True)
    dscores = (probs * (dprobs - delta) * scale).astype(jnp.bfloat16)
    query_part = jnp.einsum(out_form, dscores, keys, preferred_element_type=f32)
    key_part = jnp.einsum(back_form, dscores, queries, preferred_element_type=f32)
    return (query_part, key_part, value_part)


def unnorm(grads, values, inverse, scales):
    scaled = scales * grads
    inputs_grad = inverse * scaled - values * inverse**3 * jnp.mean(
        scaled * values, axis=-1, keepdims=True
    )
    gain_grad = jnp.sum(grads * values * inverse, axis=(0, 1))
    return (inputs_grad, gain_grad)


def make_valid(frame_ids, spot_ids, count_f, count_h, count_w):
    spot_fits = (spot_ids // PATCH_COLS < count_h) & (spot_ids % PATCH_COLS < count_w)
    return (frame_ids[:, None] < count_f) & spot_fits[None, :]


def shards(query_input, key_input, value_input, cotangent, q_gain, k_gain, frames, heights, widths):
    frame_rows = query_input.shape[1]
    spots = query_input.shape[2]
    chans = query_input.shape[3]
    heads = chans // HEAD_DIM
    seq_count = lax.axis_size("seq")
    seq_place = lax.axis_index("seq")
    gains_q, gains_k = (
        lax.all_gather(q_gain, "dp", axis=0, tiled=True),
        lax.all_gather(k_gain, "dp", axis=0, tiled=True),
    )
    count_f = frames[0]
    count_h = heights[0]
    count_w = widths[0]
    frame_ids = seq_place * frame_rows + jnp.arange(frame_rows)
    valid = make_valid(frame_ids, jnp.arange(spots), count_f, count_h, count_w)
    normed_q, values_q, inverse_q, scales_q = normalize(query_input[0], gains_q, heads)
    normed_k, values_k, inverse_k, scales_k = normalize(key_input[0], gains_k, heads)
    shape4 = (frame_rows, spots, heads, HEAD_DIM)
    masked_cot = jnp.where(
        valid[:, :, None, None], cotangent[0].reshape(shape4), jnp.zeros((), jnp.bfloat16)
    )
    values4 = value_input[0].reshape(shape4)
    line_q, line_k, line_v = (
        lax.all_to_all(normed_q, "seq", split_axis=1, concat_axis=0, tiled=True),
        lax.all_to_all(normed_k, "seq", split_axis=1, concat_axis=0, tiled=True),
        lax.all_to_all(values4, "seq", split_axis=1, concat_axis=0, tiled=True),
    )
    spatial_q, spatial_k, spatial_v = attend(normed_q, normed_k, values4, masked_cot, valid, False)
    line_c = lax.all_to_all(masked_cot, "seq", split_axis=1, concat_axis=0, tiled=True)
    line_spots = spots // seq_count
    spot_ids = seq_place * line_spots + jnp.arange(line_spots)
    valid_lines = make_valid(
        jnp.arange(frame_rows * seq_count), spot_ids, count_f, count_h, count_w
    )
    temporal_q, temporal_k, temporal_v = attend(line_q, line_k, line_v, line_c, valid_lines, True)
    back_q, back_k, back_v = (
        lax.all_to_all(
            temporal_q.astype(jnp.bfloat16), "seq", split_axis=0, concat_axis=1, tiled=True
        ),
        lax.all_to_all(
            temporal_k.astype(jnp.bfloat16), "seq", split_axis=0, concat_axis=1, tiled=True
        ),
        lax.all_to_all(
            temporal_v.astype(jnp.bfloat16), "seq", split_axis=0, concat_axis=1, tiled=True
        ),
    )
    grad_q = spatial_q + back_q.astype(jnp.float32)
    grad_k = spatial_k + back_k.astype(jnp.float32)
    value_grad = (spatial_v + back_v.astype(jnp.float32)).astype(jnp.bfloat16)
    query_grad, local_gq = unnorm(grad_q, values_q, inverse_q, scales_q)
    key_grad, local_gk = unnorm(grad_k, values_k, inverse_k, scales_k)
    local_gq = local_gq.reshape(-1)
    local_gk = local_gk.reshape(-1)
    clip_q, clip_k = lax.psum((local_gq, local_gk), "seq")
    share_q, share_k = (
        lax.psum_scatter(clip_q, "dp", scatter_dimension=0, tiled=True),
        lax.psum_scatter(clip_k, "dp", scatter_dimension=0, tiled=True),
    )
    full = (1, frame_rows, spots, chans)
    return (
        query_grad.astype(jnp.bfloat16).reshape(full),
        key_grad.astype(jnp.bfloat16).reshape(full),
        value_grad.reshape(full),
        share_q,
        share_k,
    )


def solution(mesh):
    return jax.shard_map(
        shards,
        mesh=mesh,
        in_specs=(
            P("dp", "seq", None, None),
            P("dp", "seq", None, None),
            P("dp", "seq", None, None),
            P("dp", "seq", None, None),
            P("dp"),
            P("dp"),
            P("dp"),
            P("dp"),
            P("dp"),
        ),
        out_specs=(
            P("dp", "seq", None, None),
            P("dp", "seq", None, None),
            P("dp", "seq", None, None),
            P("dp"),
            P("dp"),
        ),
        check_vma=False,
    )
```

profile of v0, /device:TPU:1, one launch (start us, length us, event | category | flops | bytes accessed | tf_op | source)
XLA Modules:
  0.0 409.2 jit_solution(6519830171116095040)
XLA Ops:
  7.3 96.8 %all-reduce.5 = (f32[1536]{0:T(1024)S(1)}, f32[1536]{0:T(1024)S(1)}) all-reduce(f32[1536]{0:T(1024)S(1)} %dynamic-update-slice.1, f32[1536]{0:T(1024)S(1)} %dynamic-update-slice), channel_id=1, replica_groups=mesh['dp'=32,'seq'=16] {'dp'}, use_global_device_ids=true, to_apply=%add.1 | all-reduce | flops 3072 | bytes 24576
  107.2 6.8 %all-to-all-start = ((bf16[1,240,12,128]{3,2,0,1:T(8,128)(2,1)}), bf16[1,240,12,128]{3,2,0,1:T(8,128)(2,1)}, u32[]{:S(2)}, u32[]{:S(2)}) async-start(bf16[1,240,12,128]{3,2,0,1:T(8,128)(2,1)} %copy.185), calls=%async_computation | async-start | bytes 1966080 | tf_op jit(solution)/shard_map/all_to_all | solution.py:86
  122.9 4.1 %all-to-all-done = bf16[1,240,12,128]{3,2,0,1:T(8,128)(2,1)} async-done(((bf16[1,240,12,128]{3,2,0,1:T(8,128)(2,1)}), bf16[1,240,12,128]{3,2,0,1:T(8,128)(2,1)}, u32[]{:S(2)}, u32[]{:S(2)}) %all-to-all-start) | async-done | bytes 737312 | tf_op jit(solution)/shard_map/all_to_all | solution.py:86
  127.0 4.3 %all-to-all-start.2 = ((bf16[1,240,12,128]{3,2,0,1:T(8,128)(2,1)}), bf16[1,240,12,128]{3,2,0,1:T(8,128)(2,1)}, u32[]{:S(2)}, u32[]{:S(2)}) async-start(bf16[1,240,12,128]{3,2,0,1:T(8,128)(2,1)} %copy.193), calls=%async_computation.2 | async-start | bytes 1966080 | tf_op jit(solution)/shard_map/all_to_all | solution.py:90
  136.1 7.5 %all-to-all-done.2 = bf16[1,240,12,128]{3,2,0,1:T(8,128)(2,1)} async-done(((bf16[1,240,12,128]{3,2,0,1:T(8,128)(2,1)}), bf16[1,240,12,128]{3,2,0,1:T(8,128)(2,1)}, u32[]{:S(2)}, u32[]{:S(2)}) %all-to-all-start.2) | async-done | bytes 737312 | tf_op jit(solution)/shard_map/all_to_all | solution.py:90
  143.6 4.3 %all-to-all-start.3 = ((bf16[1,240,12,128]{3,2,0,1:T(8,128)(2,1)}), bf16[1,240,12,128]{3,2,0,1:T(8,128)(2,1)}, u32[]{:S(2)}, u32[]{:S(2)}) async-start(bf16[1,240,12,128]{3,2,0,1:T(8,128)(2,1)} %copy.196), calls=%async_computation.3 | async-start | bytes 1966080 | tf_op jit(solution)/shard_map/all_to_all | solution.py:87
  152.6 7.5 %all-to-all-done.3 = bf16[1,240,12,128]{3,2,0,1:T(8,128)(2,1)} async-done(((bf16[1,240,12,128]{3,2,0,1:T(8,128)(2,1)}), bf16[1,240,12,128]{3,2,0,1:T(8,128)(2,1)}, u32[]{:S(2)}, u32[]{:S(2)}) %all-to-all-start.3) | async-done | bytes 737312 | tf_op jit(solution)/shard_map/all_to_all | solution.py:87
  160.1 4.3 %all-to-all-start.1 = ((bf16[1,240,12,128]{3,2,0,1:T(8,128)(2,1)}), bf16[1,240,12,128]{3,2,0,1:T(8,128)(2,1)}, u32[]{:S(2)}, u32[]{:S(2)}) async-start(bf16[1,240,12,128]{3,2,0,1:T(8,128)(2,1)} %copy.188), calls=%async_computation.1 | async-start | bytes 1966080 | tf_op jit(solution)/shard_map/all_to_all | solution.py:85
  164.5 3.2 fusion.40
  167.7 8.6 %all-to-all-done.1 = bf16[1,240,12,128]{3,2,0,1:T(8,128)(2,1)} async-done(((bf16[1,240,12,128]{3,2,0,1:T(8,128)(2,1)}), bf16[1,240,12,128]{3,2,0,1:T(8,128)(2,1)}, u32[]{:S(2)}, u32[]{:S(2)}) %all-to-all-start.1) | async-done | bytes 737312 | tf_op jit(solution)/shard_map/all_to_all | solution.py:85
  176.3 3.6 fusion.70
  179.9 4.8 %fusion.34 = bf16[16,15,12,128]{3,0,2,1:T(8,128)(2,1)} fusion(f32[15,12,16,16]{2,3,1,0:T(8,128)} %fusion.40, bf16[16,15,12,128]{3,2,1,0:T(8,128)(2,1)} %bitcast.18, f32[15,12,16,16]{2,3,1,0:T(8,128)} %get-tuple-element.42, f32[15,12,16]{2,1,0:T(8,128)S(1)} %get-tuple-element.41), kind=kOutput, calls=%fused_computation.46 | convolution fusion | flops 12490575 | bytes 1854720 | tf_op jit(solution)/shard_map/bhij,ibhd->jbhd/dot_general | solution.py:43
  187.2 4.5 %all-to-all-start.5 = ((bf16[16,15,12,128]{3,1,2,0:T(8,128)(2,1)}), bf16[16,15,12,128]{3,1,2,0:T(8,128)(2,1)}, u32[]{:S(2)}, u32[]{:S(2)}) async-start(bf16[16,15,12,128]{3,1,2,0:T(8,128)(2,1)} %copy.210), calls=%async_computation.5 | async-start | bytes 1572864 | tf_op jit(solution)/shard_map/all_to_all | solution.py:101
  193.3 2.9 fusion.71
  196.2 4.9 %fusion.33 = bf16[16,15,12,128]{3,0,2,1:T(8,128)(2,1)} fusion(f32[15,12,16,16]{2,3,1,0:T(8,128)} %fusion.40, bf16[16,15,12,128]{3,2,1,0:T(8,128)(2,1)} %bitcast.16, f32[15,12,16,16]{2,3,1,0:T(8,128)} %get-tuple-element.42, f32[15,12,16]{2,1,0:T(8,128)S(1)} %get-tuple-element.41), kind=kOutput, calls=%fused_computation.45 | convolution fusion | flops 12490575 | bytes 1854720 | tf_op jit(solution)/shard_map/bhij,jbhd->ibhd/dot_general | solution.py:42
  203.6 6.4 %all-to-all-start.4 = ((bf16[16,15,12,128]{3,1,2,0:T(8,128)(2,1)}), bf16[16,15,12,128]{3,1,2,0:T(8,128)(2,1)}, u32[]{:S(2)}, u32[]{:S(2)}) async-start(bf16[16,15,12,128]{3,1,2,0:T(8,128)(2,1)} %copy.202), calls=%async_computation.4 | async-start | bytes 1572864 | tf_op jit(solution)/shard_map/all_to_all | solution.py:98
  210.0 3.6 fusion.45
  223.9 6.7 %all-to-all-start.6 = ((bf16[16,15,12,128]{3,1,2,0:T(8,128)(2,1)}), bf16[16,15,12,128]{3,1,2,0:T(8,128)(2,1)}, u32[]{:S(2)}, u32[]{:S(2)}) async-start(bf16[16,15,12,128]{3,1,2,0:T(8,128)(2,1)} %copy.218), calls=%async_computation.6 | async-start | bytes 1572864 | tf_op jit(solution)/shard_map/all_to_all | solution.py:104
  236.7 7.2 %multiply_reduce_fusion.3 = (f32[12,128]{1,0:T(8,128)S(1)}, f32[240,12]{0,1:T(8,128)S(1)}, f32[1,240,12,128]{3,1,2,0:T(8,128)}) fusion(f32[1,240,12,128]{3,1,2,0:T(8,128)} %copy.184, f32[240,12]{0,1:T(8,128)S(1)} %get-tuple-element.36, f32[12,128]{1,0:T(8,128)S(1)} %bitcast.83, f32[1,240,12,128]{3,1,2,0:T(8,128)} %reshape.474, f32[12,240,240]{1,2,0:T(8,128)} %fusion.45, ...), kind=kOutput, calls=%fused_computation.21 | convolution fusion | flops 185470704 | bytes 11492352 | tf_op jit(solution)/shard_map/bhij,bihd->bjhd/dot_general | solution.py:43
  243.9 7.4 %multiply_reduce_fusion.4 = (f32[12,128]{1,0:T(8,128)S(1)}, f32[240,12]{0,1:T(8,128)S(1)}, f32[1,240,12,128]{3,1,2,0:T(8,128)}) fusion(f32[1,240,12,128]{3,1,2,0:T(8,128)} %copy.187, f32[240,12]{0,1:T(8,128)S(1)} %get-tuple-element.47, f32[12,128]{1,0:T(8,128)S(1)} %bitcast.79, f32[1,240,12,128]{3,1,2,0:T(8,128)} %reshape.473, f32[12,240,240]{1,2,0:T(8,128)} %fusion.45, ...), kind=kOutput, calls=%fused_computation.22 | convolution fusion | flops 185470704 | bytes 11492352 | tf_op jit(solution)/shard_map/bhij,bjhd->bihd/dot_general | solution.py:42
  251.3 106.7 %all-reduce.4 = (f32[1536]{0:T(1024)S(1)}, f32[1536]{0:T(1024)S(1)}) all-reduce(f32[1536]{0:T(1024)S(1)} %bitcast.87, f32[1536]{0:T(1024)S(1)} %bitcast.86), channel_id=2, replica_groups=mesh['dp'=32,'seq'=16] {'dp'}, use_global_device_ids=true, to_apply=%region_12.13.clone | all-reduce | flops 3072 | bytes 24576
  366.3 3.0 subtract_convert_fusion
  370.7 3.0 subtract_convert_fusion.1
  375.2 34.0 %all-reduce.6 = (f32[48]{0:T(128)}, f32[48]{0:T(128)}) all-reduce(f32[48]{0:T(128)S(1)} %dynamic-slice.3, f32[48]{0:T(128)S(1)} %dynamic-slice.5), channel_id=1, replica_groups=mesh['dp'=32,'seq'=16] {'seq'}, use_global_device_ids=true, to_apply=%region_11.12 | all-reduce | flops 96 | bytes 768 | tf_op jit(solution)/shard_map/psum | solution.py:115
  (65 shorter events, 58.9 us)
Async XLA Ops:
  3.9 1.6 copy-start.3
  3.9 2.9 copy-start.4
  3.9 3.2 copy-start.5
  107.2 19.8 %all-to-all-start = ((bf16[1,240,12,128]{3,2,0,1:T(8,128)(2,1)}), bf16[1,240,12,128]{3,2,0,1:T(8,128)(2,1)}, u32[]{:S(2)}, u32[]{:S(2)}) async-start(bf16[1,240,12,128]{3,2,0,1:T(8,128)(2,1)} %copy.185), calls=%async_computation | async-start | bytes 1966080 | tf_op jit(solution)/shard_map/all_to_all | solution.py:86
  127.0 16.6 %all-to-all-start.2 = ((bf16[1,240,12,128]{3,2,0,1:T(8,128)(2,1)}), bf16[1,240,12,128]{3,2,0,1:T(8,128)(2,1)}, u32[]{:S(2)}, u32[]{:S(2)}) async-start(bf16[1,240,12,128]{3,2,0,1:T(8,128)(2,1)} %copy.193), calls=%async_computation.2 | async-start | bytes 1966080 | tf_op jit(solution)/shard_map/all_to_all | solution.py:90
  143.6 16.5 %all-to-all-start.3 = ((bf16[1,240,12,128]{3,2,0,1:T(8,128)(2,1)}), bf16[1,240,12,128]{3,2,0,1:T(8,128)(2,1)}, u32[]{:S(2)}, u32[]{:S(2)}) async-start(bf16[1,240,12,128]{3,2,0,1:T(8,128)(2,1)} %copy.196), calls=%async_computation.3 | async-start | bytes 1966080 | tf_op jit(solution)/shard_map/all_to_all | solution.py:87
  160.1 16.2 %all-to-all-start.1 = ((bf16[1,240,12,128]{3,2,0,1:T(8,128)(2,1)}), bf16[1,240,12,128]{3,2,0,1:T(8,128)(2,1)}, u32[]{:S(2)}, u32[]{:S(2)}) async-start(bf16[1,240,12,128]{3,2,0,1:T(8,128)(2,1)} %copy.188), calls=%async_computation.1 | async-start | bytes 1966080 | tf_op jit(solution)/shard_map/all_to_all | solution.py:85
  187.2 16.4 %all-to-all-start.5 = ((bf16[16,15,12,128]{3,1,2,0:T(8,128)(2,1)}), bf16[16,15,12,128]{3,1,2,0:T(8,128)(2,1)}, u32[]{:S(2)}, u32[]{:S(2)}) async-start(bf16[16,15,12,128]{3,1,2,0:T(8,128)(2,1)} %copy.210), calls=%async_computation.5 | async-start | bytes 1572864 | tf_op jit(solution)/shard_map/all_to_all | solution.py:101
  203.6 20.3 %all-to-all-start.4 = ((bf16[16,15,12,128]{3,1,2,0:T(8,128)(2,1)}), bf16[16,15,12,128]{3,1,2,0:T(8,128)(2,1)}, u32[]{:S(2)}, u32[]{:S(2)}) async-start(bf16[16,15,12,128]{3,1,2,0:T(8,128)(2,1)} %copy.202), calls=%async_computation.4 | async-start | bytes 1572864 | tf_op jit(solution)/shard_map/all_to_all | solution.py:98
  223.9 134.3 %all-to-all-start.6 = ((bf16[16,15,12,128]{3,1,2,0:T(8,128)(2,1)}), bf16[16,15,12,128]{3,1,2,0:T(8,128)(2,1)}, u32[]{:S(2)}, u32[]{:S(2)}) async-start(bf16[16,15,12,128]{3,1,2,0:T(8,128)(2,1)} %copy.218), calls=%async_computation.6 | async-start | bytes 1572864 | tf_op jit(solution)/shard_map/all_to_all | solution.py:104
  360.6 1.4 copy-start.2
  364.9 1.4 copy-start
  369.3 1.4 copy-start.1
where the time goes:
time: 417 us; the launch traced here: 409 us
  blocking collectives  238 us (57%)
  local copies, waits for them, and re-layouts  41.4 us (10%)
  matrix products  41.3 us (10%)
  starting transfers between devices  37.3 us (9%)
  waiting for transfers between devices  27.7 us (7%)
  other arithmetic  19.8 us (5%)
    unnamed x2, blocking collectives  204 us
    psum x1, blocking collectives, shards(): clip_q, clip_k = lax.psum((local_gq, local_gk), 'seq')  34 us
    dot_general x2, matrix products, attend(): query_part = jnp.einsum(out_form, dscores, keys, preferred_element_type=f32)  12.3 us
    dot_general x2, matrix products, attend(): jnp.einsum(back_form, dscores, queries, preferred_element_type=f32)  12 us
    unnamed x24, local copies, waits for them, and re-layouts  9.4 us
    all_to_all x1, waiting for transfers between devices, shards(): lax.all_to_all(normed_q, 'seq', split_axis=1, concat_axis=0, tiled=True)  8.6 us
  transfers between devices with their start and end apart: 7, of which 4 were waited for; matrix products, arithmetic and copies ran while one was open for 16% of the time, Pallas kernels for 0%

commit v1 on v0

v1 whole, which is shorter than its diff:
```python
import functools
import math

import jax
import jax.numpy as jnp
from jax import lax
from jax.experimental import pallas as pl
from jax.experimental.pallas import tpu as pltpu
from jax.sharding import PartitionSpec as P

HEADS = 12
DIM = 128
COLS = 16
FRAMES = 16
SPOTS = 240
BLOCK = 16
CHANNELS = HEADS * DIM
EPS = 1e-06
NEGATIVE = -1e30
FAR = -2e30
SCALE = 1.0 / math.sqrt(DIM)
MESH = pl.DeviceIdType.MESH
F32 = jnp.float32
BF16 = jnp.bfloat16


def dot(a, b, dims):
    return lax.dot_general(a, b, (dims, ((), ())), preferred_element_type=F32)


def inverse_norm(values):
    return lax.rsqrt(jnp.sum(values * values, axis=-1, keepdims=True) * (1.0 / DIM) + EPS)


def attend(queries, keys, values, cotan, bias):
    scores = dot(keys, queries, ((1,), (1,))) * SCALE + bias
    top = jnp.max(scores, axis=0, keepdims=True)
    expo = jnp.exp(scores - top)
    probs = expo / jnp.sum(expo, axis=0, keepdims=True)
    dprobs = dot(values, cotan, ((1,), (1,)))
    value_part = dot(probs.astype(BF16), cotan, ((1,), (0,)))
    delta = jnp.sum(probs * dprobs, axis=0, keepdims=True)
    dscores = (probs * (dprobs - delta) * SCALE).astype(BF16)
    key_part = dot(dscores, queries, ((1,), (0,)))
    query_part = dot(dscores, keys, ((0,), (0,)))
    return query_part, key_part, value_part


def idle_of(head):
    return jnp.where(head < 11, head, 15)


def main_kernel(
    q_hbm, k_hbm, v_hbm, c_hbm, gains, frames, heights, widths,
    dq_hbm, dk_hbm, dv_hbm, gpart,
    stack, recv, tout, ret, sgrad, outs, bias_t,
    load_sem, fwd_send, fwd_recv, own_sem, back_send, back_recv, out_sem,
):
    me = lax.axis_index("seq")

    loads = [
        pltpu.make_async_copy(src, stack.at[a], load_sem.at[a])
        for a, src in enumerate((q_hbm, k_hbm, v_hbm, c_hbm))
    ]
    for load in loads:
        load.start()

    barrier = pltpu.get_barrier_semaphore()

    def greet(i, carry):
        to = lax.rem(me + i, 16)
        pl.semaphore_signal(barrier, inc=1, device_id={"seq": to}, device_id_type=MESH)
        return carry

    lax.fori_loop(1, 16, greet, 0)
    for load in loads:
        load.wait()
    pl.semaphore_wait(barrier, 15)

    def lanes(head):
        return pl.ds(pl.multiple_of(head * DIM, DIM), DIM)

    def rows(block):
        return pl.ds(pl.multiple_of(block * BLOCK, BLOCK), BLOCK)

    def send_head(head, carry):
        idle = idle_of(head)

        def send_one(i, inner):
            to = lax.rem(me + i, 16)
            block = jnp.where(to < 15, to, head)

            @pl.when(to != idle)
            def _():
                pltpu.make_async_remote_copy(
                    src_ref=stack.at[:, rows(block), lanes(head)],
                    dst_ref=recv.at[head, :, rows(me), :],
                    send_sem=fwd_send.at[head],
                    recv_sem=fwd_recv.at[head],
                    device_id={"seq": to},
                    device_id_type=MESH,
                ).start()

            return inner

        lax.fori_loop(1, 16, send_one, 0)

        @pl.when(me != idle)
        def _():
            block = jnp.where(me < 15, me, head)
            pltpu.make_async_copy(
                stack.at[:, rows(block), lanes(head)],
                recv.at[head, :, rows(me), :],
                own_sem.at[head],
            ).start()

        return carry

    lax.fori_loop(0, HEADS, send_head, 0)

    count_f, count_h, count_w = frames[0], heights[0], widths[0]

    def spot_fits(spot):
        return (spot // COLS < count_h) & (spot % COLS < count_w)

    spot = lax.broadcasted_iota(jnp.int32, (SPOTS, 1), 0)
    valid_s = spot_fits(spot) & (me < count_f)
    bias_s = jnp.where(valid_s, 0.0, NEGATIVE).astype(F32)
    cot_s = jnp.where(valid_s, 1.0, 0.0).astype(F32)

    def spatial(head, carry):
        q32 = stack[0, :, lanes(head)].astype(F32)
        k32 = stack[1, :, lanes(head)].astype(F32)
        inv_q, inv_k = inverse_norm(q32), inverse_norm(k32)
        gain_q, gain_k = gains[pl.ds(head, 1), :], gains[pl.ds(head + HEADS, 1), :]
        scaled_q, scaled_k = q32 * inv_q, k32 * inv_k
        normed_q = (scaled_q * gain_q).astype(BF16)
        normed_k = (scaled_k * gain_k).astype(BF16)
        cotan = (stack[3, :, lanes(head)].astype(F32) * cot_s).astype(BF16)
        part_q, part_k, part_v = attend(normed_q, normed_k, stack[2, :, lanes(head)], cotan, bias_s)
        sgrad[head, 0] = part_q
        sgrad[head, 1] = part_k
        sgrad[head, 2] = part_v
        gpart[pl.ds(head, 1), :] = jnp.sum(part_q * scaled_q, axis=0, keepdims=True)
        gpart[pl.ds(head + HEADS, 1), :] = jnp.sum(part_k * scaled_k, axis=0, keepdims=True)
        return carry

    lax.fori_loop(0, HEADS, spatial, 0)

    line = lax.broadcasted_iota(jnp.int32, (256, 1), 0)
    key_at = lax.broadcasted_iota(jnp.int32, (256, 256), 0)
    query_at = lax.broadcasted_iota(jnp.int32, (256, 256), 1)
    same = key_at % BLOCK == query_at % BLOCK

    def temporal(head, carry):
        idle = idle_of(head)

        @pl.when(me != idle)
        def _():
            block = jnp.where(me < 15, me, head)
            pltpu.make_async_copy(
                recv.at[head, :, pl.ds(0, 240), :], recv.at[head, :, pl.ds(0, 240), :], fwd_recv.at[head]
            ).wait()
            pltpu.make_async_copy(
                recv.at[head, :, pl.ds(0, 16), :], recv.at[head, :, pl.ds(0, 16), :], own_sem.at[head]
            ).wait()
            valid_t = spot_fits(block * BLOCK + line % BLOCK) & (line // BLOCK < count_f)
            cot_t = jnp.where(valid_t, 1.0, 0.0).astype(F32)
            bias_t[...] = jnp.where(same, jnp.where(valid_t, 0.0, NEGATIVE), FAR).astype(F32)
            q32 = recv[head, 0].astype(F32)
            k32 = recv[head, 1].astype(F32)
            inv_q, inv_k = inverse_norm(q32), inverse_norm(k32)
            gain_q, gain_k = gains[pl.ds(head, 1), :], gains[pl.ds(head + HEADS, 1), :]
            scaled_q, scaled_k = q32 * inv_q, k32 * inv_k
            normed_q = (scaled_q * gain_q).astype(BF16)
            normed_k = (scaled_k * gain_k).astype(BF16)
            cotan = (recv[head, 3].astype(F32) * cot_t).astype(BF16)
            part_q, part_k, part_v = attend(normed_q, normed_k, recv[head, 2], cotan, bias_t[...])
            part_q, part_k = part_q.astype(BF16), part_k.astype(BF16)
            tout[head, 0] = part_q
            tout[head, 1] = part_k
            tout[head, 2] = part_v.astype(BF16)

            def send_back(i, inner):
                to = lax.rem(me + i, 16)
                pltpu.make_async_remote_copy(
                    src_ref=tout.at[head, :, rows(to), :],
                    dst_ref=ret.at[head, :, rows(block), :],
                    send_sem=back_send.at[head],
                    recv_sem=back_recv.at[head],
                    device_id={"seq": to},
                    device_id_type=MESH,
                ).start()
                return inner

            lax.fori_loop(1, 16, send_back, 0)
            pltpu.make_async_copy(
                tout.at[head, :, rows(me), :], ret.at[head, :, rows(block), :], own_sem.at[head]
            ).start()
            gpart[pl.ds(head, 1), :] += jnp.sum(part_q.astype(F32) * scaled_q, axis=0, keepdims=True)
            gpart[pl.ds(head + HEADS, 1), :] += jnp.sum(
                part_k.astype(F32) * scaled_k, axis=0, keepdims=True
            )

        return carry

    lax.fori_loop(0, HEADS, temporal, 0)

    def finish(head, carry):
        idle = idle_of(head)

        @pl.when(me != idle)
        def _():
            pltpu.make_async_copy(
                ret.at[head, :, pl.ds(0, 224), :], ret.at[head, :, pl.ds(0, 224), :], back_recv.at[head]
            ).wait()
            pltpu.make_async_copy(
                ret.at[head, :, pl.ds(0, 16), :], ret.at[head, :, pl.ds(0, 16), :], own_sem.at[head]
            ).wait()

        @pl.when(me == idle)
        def _():
            pltpu.make_async_copy(ret.at[head], ret.at[head], back_recv.at[head]).wait()

        for a in range(2):
            raw = stack[a, :, lanes(head)].astype(F32)
            inverse = inverse_norm(raw)
            gain = gains[pl.ds(head + HEADS * a, 1), :]
            scaled = gain * (sgrad[head, a] + ret[head, a].astype(F32))
            mean = jnp.sum(scaled * raw, axis=-1, keepdims=True) * (1.0 / DIM)
            outs[a, :, lanes(head)] = (
                inverse * scaled - raw * (inverse * inverse * inverse) * mean
            ).astype(BF16)
        outs[2, :, lanes(head)] = (sgrad[head, 2] + ret[head, 2].astype(F32)).astype(BF16)
        for a, dst in enumerate((dq_hbm, dk_hbm, dv_hbm)):
            pltpu.make_async_copy(
                outs.at[a, :, lanes(head)], dst.at[:, lanes(head)], out_sem.at[a]
            ).start()
        return carry

    lax.fori_loop(0, HEADS, finish, 0)

    def drain(head, carry):
        idle = idle_of(head)

        @pl.when(me != idle)
        def _():
            pltpu.make_async_copy(
                recv.at[head, :, pl.ds(0, 224), :], recv.at[head, :, pl.ds(0, 224), :], fwd_send.at[head]
            ).wait()
            pltpu.make_async_copy(
                tout.at[head, :, pl.ds(0, 240), :], tout.at[head, :, pl.ds(0, 240), :], back_send.at[head]
            ).wait()

        @pl.when(me == idle)
        def _():
            pltpu.make_async_copy(
                recv.at[head, :, pl.ds(0, 240), :], recv.at[head, :, pl.ds(0, 240), :], fwd_send.at[head]
            ).wait()

        return carry

    lax.fori_loop(0, HEADS, drain, 0)
    for a, dst in enumerate((dq_hbm, dk_hbm, dv_hbm)):
        pltpu.make_async_copy(outs.at[a], dst, out_sem.at[a]).wait()


def main_call(q, k, v, c, gains, frames, heights, widths):
    any_spec = pl.BlockSpec(memory_space=pltpu.HBM)
    vmem = pl.BlockSpec(memory_space=pltpu.VMEM)
    smem = pl.BlockSpec(memory_space=pltpu.SMEM)
    grad = jax.ShapeDtypeStruct((SPOTS, CHANNELS), BF16)
    return pl.pallas_call(
        main_kernel,
        out_shape=(grad, grad, grad, jax.ShapeDtypeStruct((2 * HEADS, DIM), F32)),
        in_specs=[any_spec] * 4 + [vmem] + [smem] * 3,
        out_specs=(any_spec, any_spec, any_spec, vmem),
        scratch_shapes=[
            pltpu.VMEM((4, SPOTS, CHANNELS), BF16),
            pltpu.VMEM((HEADS, 4, 256, DIM), BF16),
            pltpu.VMEM((HEADS, 3, 256, DIM), BF16),
            pltpu.VMEM((HEADS, 3, SPOTS, DIM), BF16),
            pltpu.VMEM((HEADS, 3, SPOTS, DIM), F32),
            pltpu.VMEM((3, SPOTS, CHANNELS), BF16),
            pltpu.VMEM((256, 256), F32),
            pltpu.SemaphoreType.DMA((4,)),
            pltpu.SemaphoreType.DMA((HEADS,)),
            pltpu.SemaphoreType.DMA((HEADS,)),
            pltpu.SemaphoreType.DMA((HEADS,)),
            pltpu.SemaphoreType.DMA((HEADS,)),
            pltpu.SemaphoreType.DMA((HEADS,)),
            pltpu.SemaphoreType.DMA((3,)),
        ],
        compiler_params=pltpu.CompilerParams(
            collective_id=1, has_side_effects=True, vmem_limit_bytes=40 << 20
        ),
        name="axial",
    )(q, k, v, c, gains, frames, heights, widths)


def greet_all(barrier, axis, size):
    me = lax.axis_index(axis)

    def greet(i, carry):
        to = lax.rem(me + i, size)
        pl.semaphore_signal(barrier, inc=1, device_id={axis: to}, device_id_type=MESH)
        return carry

    lax.fori_loop(1, size, greet, 0)


def piece_of(i, count, size):
    start = i * size
    return start // DIM, start % DIM, start % DIM + size > DIM


def gather_kernel(count, size, q_ref, k_ref, gains, mine, held, send_sem, recv_sem):
    me = lax.axis_index("dp")
    barrier = pltpu.get_barrier_semaphore()
    greet_all(barrier, "dp", count)
    mine[...] = jnp.zeros_like(mine)
    mine[0:1, 0:size] = q_ref[...]
    mine[1:2, 0:size] = k_ref[...]
    mine[...] = pltpu.roll(mine[...], lax.rem(me * size, DIM), 1)
    held[me] = mine[...]
    pl.semaphore_wait(barrier, count - 1)

    def send(i, carry):
        to = lax.rem(me + i, count)
        pltpu.make_async_remote_copy(
            src_ref=mine,
            dst_ref=held.at[me],
            send_sem=send_sem,
            recv_sem=recv_sem,
            device_id={"dp": to},
            device_id_type=MESH,
        ).start()
        return carry

    lax.fori_loop(1, count, send, 0)
    others = held.at[pl.ds(0, count - 1)]
    pltpu.make_async_copy(others, others, recv_sem).wait()
    pltpu.make_async_copy(others, others, send_sem).wait()
    lane = lax.broadcasted_iota(jnp.int32, (8, DIM), 1)
    total = [jnp.zeros((8, DIM), F32) for _ in range(HEADS)]
    for i in range(count):
        head, off, spills = piece_of(i, count, size)
        tile = held[i]
        total[head] += jnp.where(lane >= off, tile, 0.0)
        if spills:
            total[head + 1] += jnp.where(lane < off, tile, 0.0)
    for head in range(HEADS):
        gains[head : head + 1, :] = total[head][0:1]
        gains[head + HEADS : head + HEADS + 1, :] = total[head][1:2]


def gather_gains(q_gain, k_gain, count):
    size = q_gain.shape[0]
    vmem = pl.BlockSpec(memory_space=pltpu.VMEM)
    return pl.pallas_call(
        functools.partial(gather_kernel, count, size),
        out_shape=jax.ShapeDtypeStruct((2 * HEADS, DIM), F32),
        in_specs=[vmem, vmem],
        out_specs=vmem,
        scratch_shapes=[
            pltpu.VMEM((8, DIM), F32),
            pltpu.VMEM((count, 8, DIM), F32),
            pltpu.SemaphoreType.DMA,
            pltpu.SemaphoreType.DMA,
        ],
        compiler_params=pltpu.CompilerParams(collective_id=2, has_side_effects=True),
        name="gather_gains",
    )(q_gain.reshape(1, size), k_gain.reshape(1, size))


def reduce_kernel(
    count, size, gpart, q_out, k_out, cut, held, mine, line, send_sem, recv_sem, send2_sem, recv2_sem
):
    me = lax.axis_index("dp")
    place = lax.axis_index("seq")
    barrier = pltpu.get_barrier_semaphore()
    greet_all(barrier, "dp", count)
    greet_all(barrier, "seq", FRAMES)
    lane = lax.broadcasted_iota(jnp.int32, (1, DIM), 1)
    cut[...] = jnp.zeros_like(cut)
    for i in range(count):
        head, off, spills = piece_of(i, count, size)
        for a in range(2):
            at = head + a * HEADS
            row = gpart[at : at + 1, :]
            if spills:
                row = jnp.where(lane >= off, row, gpart[at + 1 : at + 2, :])
            cut[i, a : a + 1, :] = row
    held[me] = cut[me]
    pl.semaphore_wait(barrier, count - 1 + FRAMES - 1)

    def send(i, carry):
        to = lax.rem(me + i, count)
        pltpu.make_async_remote_copy(
            src_ref=cut.at[to],
            dst_ref=held.at[me],
            send_sem=send_sem,
            recv_sem=recv_sem,
            device_id={"dp": to},
            device_id_type=MESH,
        ).start()
        return carry

    lax.fori_loop(1, count, send, 0)
    others = held.at[pl.ds(0, count - 1)]
    pltpu.make_async_copy(others, others, recv_sem).wait()
    mine[...] = pltpu.roll(
        jnp.sum(held[...], axis=0), lax.rem(DIM - lax.rem(me * size, DIM), DIM), 1
    )
    line[place] = mine[...]

    def share(i, carry):
        to = lax.rem(place + i, FRAMES)
        pltpu.make_async_remote_copy(
            src_ref=mine,
            dst_ref=line.at[place],
            send_sem=send2_sem,
            recv_sem=recv2_sem,
            device_id={"seq": to},
            device_id_type=MESH,
        ).start()
        return carry

    lax.fori_loop(1, FRAMES, share, 0)
    pltpu.make_async_copy(others, others, send_sem).wait()
    others2 = line.at[pl.ds(0, FRAMES - 1)]
    pltpu.make_async_copy(others2, others2, recv2_sem).wait()
    pltpu.make_async_copy(others2, others2, send2_sem).wait()
    total = jnp.sum(line[...], axis=0)
    q_out[...] = total[0:1, 0:size]
    k_out[...] = total[1:2, 0:size]


def reduce_gains(gpart, count):
    size = CHANNELS // count
    vmem = pl.BlockSpec(memory_space=pltpu.VMEM)
    share = jax.ShapeDtypeStruct((1, size), F32)
    share_q, share_k = pl.pallas_call(
        functools.partial(reduce_kernel, count, size),
        out_shape=(share, share),
        in_specs=[vmem],
        out_specs=(vmem, vmem),
        scratch_shapes=[
            pltpu.VMEM((count, 8, DIM), F32),
            pltpu.VMEM((count, 8, DIM), F32),
            pltpu.VMEM((8, DIM), F32),
            pltpu.VMEM((FRAMES, 8, DIM), F32),
            pltpu.SemaphoreType.DMA,
            pltpu.SemaphoreType.DMA,
            pltpu.SemaphoreType.DMA,
            pltpu.SemaphoreType.DMA,
        ],
        compiler_params=pltpu.CompilerParams(collective_id=3, has_side_effects=True),
        name="reduce_gains",
    )(gpart)
    return share_q.reshape(size), share_k.reshape(size)


def shards(query_input, key_input, value_input, cotangent, q_gain, k_gain, frames, heights, widths):
    count = lax.axis_size("dp")
    flat = (SPOTS, CHANNELS)
    gains = gather_gains(q_gain, k_gain, count)
    query_grad, key_grad, value_grad, gpart = main_call(
        query_input.reshape(flat),
        key_input.reshape(flat),
        value_input.reshape(flat),
        cotangent.reshape(flat),
        gains,
        frames,
        heights,
        widths,
    )
    share_q, share_k = reduce_gains(gpart, count)
    full = (1, 1, SPOTS, CHANNELS)
    return (
        query_grad.reshape(full),
        key_grad.reshape(full),
        value_grad.reshape(full),
        share_q,
        share_k,
    )


def solution(mesh):
    tokens = P("dp", "seq", None, None)
    return jax.shard_map(
        shards,
        mesh=mesh,
        in_specs=(tokens,) * 4 + (P("dp"),) * 5,
        out_specs=(tokens,) * 3 + (P("dp"),) * 2,
        check_vma=False,
    )
```

time: 417 us -> 127 us (0.30); the launches traced: 409 us -> 126 us
  blocking collectives: 238 us -> 0 us
  Pallas kernels: 0 us -> 115 us
  matrix products: 41.3 us -> 0 us
  starting transfers between devices: 37.3 us -> 0 us
  local copies, waits for them, and re-layouts: 41.4 us -> 8.78 us
  waiting for transfers between devices: 27.7 us -> 0 us
  other arithmetic: 19.8 us -> 0 us
    unnamed x2 -> x0, blocking collectives: 204 us -> none
    pallas_call x0 -> x3, Pallas kernels: none -> 115 us  [the longest x1 66 us: main_call(): pl.pallas_call(main_kernel, out_shape=(grad, grad, grad, jax.ShapeDtypeSt...]
    dot_general x9 -> x0, matrix products: 37.7 us -> none  [the longest x2 12.3 us: attend(): query_part = jnp.einsum(out_form, dscores, keys, preferred_element_type=f32)]
    all_to_all x7 -> x0, starting transfers between devices: 37.3 us -> none  [the longest x1 6.8 us: shards(): lax.all_to_all(normed_k, 'seq', split_axis=1, concat_axis=0, tiled=True)]
    psum x1 -> x0, blocking collectives: 34 us -> none  [shards(): clip_q, clip_k = lax.psum((local_gq, local_gk), 'seq')]
    all_to_all x7 -> x0, waiting for transfers between devices: 27.7 us -> none  [the longest x1 8.6 us: shards(): lax.all_to_all(normed_q, 'seq', split_axis=1, concat_axis=0, tiled=True)]
    convert_element_type x18 -> x0, local copies, waits for them, and re-layouts: 26.8 us -> none  [the longest x4 6.11 us: normalize(): inputs.astype(jnp.float32)]
    convert_element_type x7 -> x0, other arithmetic: 14.4 us -> none  [the longest x2 3.64 us: normalize(): (values * inverse * scales).astype(jnp.bfloat16)]
  transfers between devices with their start and end apart: 7 -> 0, of which waited for: 4 -> 0; matrix products, arithmetic and copies ran while one was open for 16% -> 0% of each run, Pallas kernels for 0% -> 0%
where the time goes in v1:
time: 127 us; the launch traced here: 126 us
  Pallas kernels  115 us (91%)
  local copies, waits for them, and re-layouts  8.78 us (7%)
  between operations  2.65 us (2%)
    pallas_call x1, Pallas kernels, main_call(): pl.pallas_call(main_kernel, out_shape=(grad, grad, grad, jax.ShapeDtypeSt...  66 us
    pallas_call x1, Pallas kernels, gather_gains(): pl.pallas_call(functools.partial(gather_kernel, count, size), out_shape=j...  24.7 us
    pallas_call x1, Pallas kernels, reduce_gains(): pl.pallas_call(functools.partial(reduce_kernel, count, size), out_shape=(...  24 us
    unnamed x21, local copies, waits for them, and re-layouts  8.78 us

profile of v1, /device:TPU:1, one launch (start us, length us, event | category | flops | bytes accessed | tf_op | source)
XLA Modules:
  0.0 126.1 jit_solution(13727803453818600766)
XLA Ops:
  0.6 24.7 %gather_gains.1.gains = f32[24,128]{1,0:T(8,128)} custom-call(f32[1,48]{1,0:T(1,128)} %bitcast.18, f32[1,48]{1,0:T(1,128)} %bitcast.19), custom_call_target="tpu_custom_call" | custom-call | tf_op jit(solution)/shard_map/gather_gains/pallas_call | solution.py:360
  25.3 0.0 copy-start.4
  27.3 0.0 copy-done.4
  27.3 0.0 copy-start
  27.3 1.1 copy-done
  28.4 0.0 copy-start.1
  28.4 1.1 copy-done.1
  29.5 0.0 copy-start.2
  29.5 1.1 copy-done.2
  30.6 0.0 copy-start.3
  30.6 1.1 copy-done.3
  31.8 66.0 %axial.1 = (bf16[240,1536]{1,0:T(8,128)(2,1)S(1)}, bf16[240,1536]{1,0:T(8,128)(2,1)S(1)}, bf16[240,1536]{1,0:T(8,128)(2,1)S(1)}, f32[24,128]{1,0:T(8,128)S(1)}) custom-call(bf16[240,1536]{1,0:T(8,128)(2,1)S(1)} %bitcast.11, bf16[240,1536]{1,0:T(8,128)(2,1)S(1)} %bitcast.12, bf16[240,1536]{1,0:T(8,128)(2,1)S(1)} %bitcast.13, bf16[240,1536]{1,0:T(8,128)(2,1)S(1)} %bitcast.14, ...), custom_call_target="tpu_custom_call" | custom-call | tf_op jit(solution)/shard_map/axial/pallas_call | solution.py:273
  97.7 0.0 copy-start.5
  97.7 0.6 copy-done.5
  98.3 24.0 %reduce_gains.1 = (f32[1,48]{1,0:T(1,128)}, f32[1,48]{1,0:T(1,128)}) custom-call(f32[24,128]{1,0:T(8,128)} %copy-done.5), custom_call_target="tpu_custom_call" | custom-call | tf_op jit(solution)/shard_map/reduce_gains/pallas_call | solution.py:443
  122.4 0.9 copy.22
  123.2 0.9 copy.23
  124.1 0.0 copy-start.7
  124.1 0.9 copy.24
  125.0 0.0 copy-done.7
  125.0 0.0 copy-start.6
  125.0 0.5 copy.25
  125.5 0.1 copy-done.6
  125.6 0.5 copy.26
Async XLA Ops:
  25.3 2.0 %copy-start.4 = (f32[24,128]{1,0:T(8,128)S(1)}, f32[24,128]{1,0:T(8,128)}, u32[]{:S(2)}) copy-start(f32[24,128]{1,0:T(8,128)} %gather_gains.1.gains) | copy-start | bytes 36868
  27.3 1.1 copy-start
  28.4 1.1 copy-start.1
  29.5 1.1 copy-start.2
  30.6 1.1 copy-start.3
  97.7 0.6 copy-start.5
  124.1 0.9 copy-start.7
  125.0 0.6 copy-start.6

commit v2 on v1

--- a/solution.py
+++ b/solution.py
@@ -50,13 +50,31 @@
     return jnp.where(head < 11, head, 15)
 
 
+def piece_of(i, size):
+    start = i * size
+    return start // DIM, start % DIM, start % DIM + size > DIM
+
+
+def greet_all(barrier, axis, size):
+    me = lax.axis_index(axis)
+
+    def greet(i, carry):
+        to = lax.rem(me + i, size)
+        pl.semaphore_signal(barrier, inc=1, device_id={axis: to}, device_id_type=MESH)
+        return carry
+
+    lax.fori_loop(1, size, greet, 0)
+
+
 def main_kernel(
-    q_hbm, k_hbm, v_hbm, c_hbm, gains, frames, heights, widths,
-    dq_hbm, dk_hbm, dv_hbm, gpart,
-    stack, recv, tout, ret, sgrad, outs, bias_t,
-    load_sem, fwd_send, fwd_recv, own_sem, back_send, back_recv, out_sem,
+    count, size,
+    q_hbm, k_hbm, v_hbm, c_hbm, q_gain, k_gain, frames, heights, widths,
+    dq_hbm, dk_hbm, dv_hbm, share_q, share_k,
+    stack, recv, tout, ret, sgrad, outs, bias_t, gains, gpart, piece, pieces, cut, cuts, sums, shares,
+    load_sem, fwd_send, fwd_recv, own_sem, back_send, back_recv, out_sem, gain_sem,
 ):
     me = lax.axis_index("seq")
+    clip = lax.axis_index("dp")
 
     loads = [
         pltpu.make_async_copy(src, stack.at[a], load_sem.at[a])
@@ -66,16 +84,18 @@
         load.start()
 
     barrier = pltpu.get_barrier_semaphore()
-
-    def greet(i, carry):
-        to = lax.rem(me + i, 16)
-        pl.semaphore_signal(barrier, inc=1, device_id={"seq": to}, device_id_type=MESH)
-        return carry
-
-    lax.fori_loop(1, 16, greet, 0)
+    greet_all(barrier, "seq", FRAMES)
+    greet_all(barrier, "dp", count)
+
+    piece[...] = jnp.zeros_like(piece)
+    piece[0:1, 0:size] = q_gain[...]
+    piece[1:2, 0:size] = k_gain[...]
+    piece[...] = pltpu.roll(piece[...], lax.rem(clip * size, DIM), 1)
+    pieces[clip] = piece[...]
+
     for load in loads:
         load.wait()
-    pl.semaphore_wait(barrier, 15)
+    pl.semaphore_wait(barrier, FRAMES - 1 + count - 1)
 
     def lanes(head):
         return pl.ds(pl.multiple_of(head * DIM, DIM), DIM)
@@ -116,7 +136,35 @@
 
         return carry
 
-    lax.fori_loop(0, HEADS, send_head, 0)
+    lax.fori_loop(0, 2, send_head, 0)
+
+    def send_piece(i, carry):
+        pltpu.make_async_remote_copy(
+            src_ref=piece,
+            dst_ref=pieces.at[clip],
+            send_sem=gain_sem.at[0],
+            recv_sem=gain_sem.at[1],
+            device_id={"dp": lax.rem(clip + i, count)},
+            device_id_type=MESH,
+        ).start()
+        return carry
+
+    lax.fori_loop(1, count, send_piece, 0)
+    lax.fori_loop(2, HEADS, send_head, 0)
+
+    others = pieces.at[pl.ds(0, count - 1)]
+    pltpu.make_async_copy(others, others, gain_sem.at[1]).wait()
+    lane = lax.broadcasted_iota(jnp.int32, (8, DIM), 1)
+    total = [jnp.zeros((8, DIM), F32) for _ in range(HEADS)]
+    for i in range(count):
+        at, off, spills = piece_of(i, size)
+        tile = pieces[i]
+        total[at] += jnp.where(lane >= off, tile, 0.0)
+        if spills:
+            total[at + 1] += jnp.where(lane < off, tile, 0.0)
+    for at in range(HEADS):
+        gains[at : at + 1, :] = total[at][0:1]
+        gains[at + HEADS : at + HEADS + 1, :] = total[at][1:2]
 
     count_f, count_h, count_w = frames[0], heights[0], widths[0]
 
@@ -206,6 +254,32 @@
 
     lax.fori_loop(0, HEADS, temporal, 0)
 
+    cut[...] = jnp.zeros_like(cut)
+    for i in range(count):
+        at, off, spills = piece_of(i, size)
+        for a in range(2):
+            row = gpart[at + a * HEADS : at + a * HEADS + 1, :]
+            if spills:
+                row = jnp.where(
+                    lane[0:1] >= off, row, gpart[at + a * HEADS + 1 : at + a * HEADS + 2, :]
+                )
+            cut[i, a : a + 1, :] = row
+    cuts[clip] = cut[clip]
+
+    def send_cut(i, carry):
+        to = lax.rem(clip + i, count)
+        pltpu.make_async_remote_copy(
+            src_ref=cut.at[to],
+            dst_ref=cuts.at[clip],
+            send_sem=gain_sem.at[2],
+            recv_sem=gain_sem.at[3],
+            device_id={"dp": to},
+            device_id_type=MESH,
+        ).start()
+        return carry
+
+    lax.fori_loop(1, count, send_cut, 0)
+
     def finish(head, carry):
         idle = idle_of(head)
 
@@ -238,7 +312,35 @@
             ).start()
         return carry
 
-    lax.fori_loop(0, HEADS, finish, 0)
+    lax.fori_loop(0, HEADS // 2, finish, 0)
+
+    others = cuts.at[pl.ds(0, count - 1)]
+    pltpu.make_async_copy(others, others, gain_sem.at[3]).wait()
+    sums[...] = pltpu.roll(
+        jnp.sum(cuts[...], axis=0), lax.rem(DIM - lax.rem(clip * size, DIM), DIM), 1
+    )
+    shares[me] = sums[...]
+
+    def send_sums(i, carry):
+        pltpu.make_async_remote_copy(
+            src_ref=sums,
+            dst_ref=shares.at[me],
+            send_sem=gain_sem.at[4],
+            recv_sem=gain_sem.at[5],
+            device_id={"seq": lax.rem(me + i, FRAMES)},
+            device_id_type=MESH,
+        ).start()
+        return carry
+
+    lax.fori_loop(1, FRAMES, send_sums, 0)
+
+    lax.fori_loop(HEADS // 2, HEADS, finish, 0)
+
+    others = shares.at[pl.ds(0, FRAMES - 1)]
+    pltpu.make_async_copy(others, others, gain_sem.at[5]).wait()
+    summed = jnp.sum(shares[...], axis=0)
+    share_q[...] = summed[0:1, 0:size]
+    share_k[...] = summed[1:2, 0:size]
 
     def drain(head, carry):
         idle = idle_of(head)
@@ -261,20 +363,28 @@
         return carry
 
     lax.fori_loop(0, HEADS, drain, 0)
+    others = cuts.at[pl.ds(0, count - 1)]
+    pltpu.make_async_copy(others, others, gain_sem.at[0]).wait()
+    pltpu.make_async_copy(others, others, gain_sem.at[2]).wait()
+    others = shares.at[pl.ds(0, FRAMES - 1)]
+    pltpu.make_async_copy(others, others, gain_sem.at[4]).wait()
     for a, dst in enumerate((dq_hbm, dk_hbm, dv_hbm)):
         pltpu.make_async_copy(outs.at[a], dst, out_sem.at[a]).wait()
 
 
-def main_call(q, k, v, c, gains, frames, heights, widths):
-    any_spec = pl.BlockSpec(memory_space=pltpu.HBM)
+def main_call(q, k, v, c, q_gain, k_gain, frames, heights, widths, count):
+    size = q_gain.shape[0]
+    any_spec = pl.BlockSpec(memory_space=pl.ANY)
     vmem = pl.BlockSpec(memory_space=pltpu.VMEM)
     smem = pl.BlockSpec(memory_space=pltpu.SMEM)
     grad = jax.ShapeDtypeStruct((SPOTS, CHANNELS), BF16)
+    share = jax.ShapeDtypeStruct((1, size), F32)
+    arrays = [pltpu.with_memory_space_constraint(x, pltpu.HBM) for x in (q, k, v, c)]
     return pl.pallas_call(
-        main_kernel,
-        out_shape=(grad, grad, grad, jax.ShapeDtypeStruct((2 * HEADS, DIM), F32)),
-        in_specs=[any_spec] * 4 + [vmem] + [smem] * 3,
-        out_specs=(any_spec, any_spec, any_spec, vmem),
+        functools.partial(main_kernel, count, size),
+        out_shape=(grad, grad, grad, share, share),
+        in_specs=[any_spec] * 4 + [vmem] * 2 + [smem] * 3,
+        out_specs=(any_spec, any_spec, any_spec, vmem, vmem),
         scratch_shapes=[
             pltpu.VMEM((4, SPOTS, CHANNELS), BF16),
             pltpu.VMEM((HEADS, 4, 256, DIM), BF16),
@@ -283,6 +393,14 @@
             pltpu.VMEM((HEADS, 3, SPOTS, DIM), F32),
             pltpu.VMEM((3, SPOTS, CHANNELS), BF16),
             pltpu.VMEM((256, 256), F32),
+            pltpu.VMEM((2 * HEADS, DIM), F32),
+            pltpu.VMEM((2 * HEADS, DIM), F32),
+            pltpu.VMEM((8, DIM), F32),
+            pltpu.VMEM((count, 8, DIM), F32),
+            pltpu.VMEM((count, 8, DIM), F32),
+            pltpu.VMEM((count, 8, DIM), F32),
+            pltpu.VMEM((8, DIM), F32),
+            pltpu.VMEM((FRAMES, 8, DIM), F32),
             pltpu.SemaphoreType.DMA((4,)),
             pltpu.SemaphoreType.DMA((HEADS,)),
             pltpu.SemaphoreType.DMA((HEADS,)),
@@ -290,199 +408,65 @@
             pltpu.SemaphoreType.DMA((HEADS,)),
             pltpu.SemaphoreType.DMA((HEADS,)),
             pltpu.SemaphoreType.DMA((3,)),
+            pltpu.SemaphoreType.DMA((6,)),
         ],
         compiler_params=pltpu.CompilerParams(
             collective_id=1, has_side_effects=True, vmem_limit_bytes=40 << 20
         ),
         name="axial",
-    )(q, k, v, c, gains, frames, heights, widths)
-
-
-def greet_all(barrier, axis, size):
-    me = lax.axis_index(axis)
-
-    def greet(i, carry):
-        to = lax.rem(me + i, size)
-        pl.semaphore_signal(barrier, inc=1, device_id={axis: to}, device_id_type=MESH)
-        return carry
-
-    lax.fori_loop(1, size, greet, 0)
-
-
-def piece_of(i, count, size):
-    start = i * size
-    return start // DIM, start % DIM, start % DIM + size > DIM
-
-
-def gather_kernel(count, size, q_ref, k_ref, gains, mine, held, send_sem, recv_sem):
-    me = lax.axis_index("dp")
-    barrier = pltpu.get_barrier_semaphore()
-    greet_all(barrier, "dp", count)
-    mine[...] = jnp.zeros_like(mine)
-    mine[0:1, 0:size] = q_ref[...]
-    mine[1:2, 0:size] = k_ref[...]
-    mine[...] = pltpu.roll(mine[...], lax.rem(me * size, DIM), 1)
-    held[me] = mine[...]
-    pl.semaphore_wait(barrier, count - 1)
-
-    def send(i, carry):
-        to = lax.rem(me + i, count)
-        pltpu.make_async_remote_copy(
-            src_ref=mine,
-            dst_ref=held.at[me],
-            send_sem=send_sem,
-            recv_sem=recv_sem,
-            device_id={"dp": to},
-            device_id_type=MESH,
-        ).start()
-        return carry
-
-    lax.fori_loop(1, count, send, 0)
-    others = held.at[pl.ds(0, count - 1)]
-    pltpu.make_async_copy(others, others, recv_sem).wait()
-    pltpu.make_async_copy(others, others, send_sem).wait()
-    lane = lax.broadcasted_iota(jnp.int32, (8, DIM), 1)
-    total = [jnp.zeros((8, DIM), F32) for _ in range(HEADS)]
-    for i in range(count):
-        head, off, spills = piece_of(i, count, size)
-        tile = held[i]
-        total[head] += jnp.where(lane >= off, tile, 0.0)
-        if spills:
-            total[head + 1] += jnp.where(lane < off, tile, 0.0)
-    for head in range(HEADS):
-        gains[head : head + 1, :] = total[head][0:1]
-        gains[head + HEADS : head + HEADS + 1, :] = total[head][1:2]
-
-
-def gather_gains(q_gain, k_gain, count):
-    size = q_gain.shape[0]
+    )(*arrays, q_gain.reshape(1, size), k_gain.reshape(1, size), frames, heights, widths)
+
+
+def emit_kernel(*refs):
+    half = len(refs) // 2
+    sem = refs[-1]
+    copies = [
+        pltpu.make_async_copy(src, dst, sem.at[i])
+        for i, (src, dst) in enumerate(zip(refs[:half], refs[half:-1]))
+    ]
+    for copy in copies:
+        copy.start()
+    for copy in copies:
+        copy.wait()
+
+
+def emit(arrays):
+    any_spec = pl.BlockSpec(memory_space=pl.ANY)
     vmem = pl.BlockSpec(memory_space=pltpu.VMEM)
     return pl.pallas_call(
-        functools.partial(gather_kernel, count, size),
-        out_shape=jax.ShapeDtypeStruct((2 * HEADS, DIM), F32),
-        in_specs=[vmem, vmem],
-        out_specs=vmem,
-        scratch_shapes=[
-            pltpu.VMEM((8, DIM), F32),
-            pltpu.VMEM((count, 8, DIM), F32),
-            pltpu.SemaphoreType.DMA,
-            pltpu.SemaphoreType.DMA,
-        ],
-        compiler_params=pltpu.CompilerParams(collective_id=2, has_side_effects=True),
-        name="gather_gains",
-    )(q_gain.reshape(1, size), k_gain.reshape(1, size))
-
-
-def reduce_kernel(
-    count, size, gpart, q_out, k_out, cut, held, mine, line, send_sem, recv_sem, send2_sem, recv2_sem
-):
-    me = lax.axis_index("dp")
-    place = lax.axis_index("seq")
-    barrier = pltpu.get_barrier_semaphore()
-    greet_all(barrier, "dp", count)
-    greet_all(barrier, "seq", FRAMES)
-    lane = lax.broadcasted_iota(jnp.int32, (1, DIM), 1)
-    cut[...] = jnp.zeros_like(cut)
-    for i in range(count):
-        head, off, spills = piece_of(i, count, size)
-        for a in range(2):
-            at = head + a * HEADS
-            row = gpart[at : at + 1, :]
-            if spills:
-                row = jnp.where(lane >= off, row, gpart[at + 1 : at + 2, :])
-            cut[i, a : a + 1, :] = row
-    held[me] = cut[me]
-    pl.semaphore_wait(barrier, count - 1 + FRAMES - 1)
-
-    def send(i, carry):
-        to = lax.rem(me + i, count)
-        pltpu.make_async_remote_copy(
-            src_ref=cut.at[to],
-            dst_ref=held.at[me],
-            send_sem=send_sem,
-            recv_sem=recv_sem,
-            device_id={"dp": to},
-            device_id_type=MESH,
-        ).start()
-        return carry
-
-    lax.fori_loop(1, count, send, 0)
-    others = held.at[pl.ds(0, count - 1)]
-    pltpu.make_async_copy(others, others, recv_sem).wait()
-    mine[...] = pltpu.roll(
-        jnp.sum(held[...], axis=0), lax.rem(DIM - lax.rem(me * size, DIM), DIM), 1
-    )
-    line[place] = mine[...]
-
-    def share(i, carry):
-        to = lax.rem(place + i, FRAMES)
-        pltpu.make_async_remote_copy(
-            src_ref=mine,
-            dst_ref=line.at[place],
-            send_sem=send2_sem,
-            recv_sem=recv2_sem,
-            device_id={"seq": to},
-            device_id_type=MESH,
-        ).start()
-        return carry
-
-    lax.fori_loop(1, FRAMES, share, 0)
-    pltpu.make_async_copy(others, others, send_sem).wait()
-    others2 = line.at[pl.ds(0, FRAMES - 1)]
-    pltpu.make_async_copy(others2, others2, recv2_sem).wait()
-    pltpu.make_async_copy(others2, others2, send2_sem).wait()
-    total = jnp.sum(line[...], axis=0)
-    q_out[...] = total[0:1, 0:size]
-    k_out[...] = total[1:2, 0:size]
-
-
-def reduce_gains(gpart, count):
-    size = CHANNELS // count
-    vmem = pl.BlockSpec(memory_space=pltpu.VMEM)
-    share = jax.ShapeDtypeStruct((1, size), F32)
-    share_q, share_k = pl.pallas_call(
-        functools.partial(reduce_kernel, count, size),
-        out_shape=(share, share),
-        in_specs=[vmem],
-        out_specs=(vmem, vmem),
-        scratch_shapes=[
-            pltpu.VMEM((count, 8, DIM), F32),
-            pltpu.VMEM((count, 8, DIM), F32),
-            pltpu.VMEM((8, DIM), F32),
-            pltpu.VMEM((FRAMES, 8, DIM), F32),
-            pltpu.SemaphoreType.DMA,
-            pltpu.SemaphoreType.DMA,
-            pltpu.SemaphoreType.DMA,
-            pltpu.SemaphoreType.DMA,
-        ],
-        compiler_params=pltpu.CompilerParams(collective_id=3, has_side_effects=True),
-        name="reduce_gains",
-    )(gpart)
-    return share_q.reshape(size), share_k.reshape(size)
+        emit_kernel,
+        out_shape=tuple(jax.ShapeDtypeStruct(x.shape, x.dtype) for x in arrays),
+        in_specs=[vmem] * len(arrays),
+        out_specs=(any_spec,) * len(arrays),
+        scratch_shapes=[pltpu.SemaphoreType.DMA((len(arrays),))],
+        compiler_params=pltpu.CompilerParams(vmem_limit_bytes=8 << 20),
+        name="emit",
+    )(*arrays)
 
 
 def shards(query_input, key_input, value_input, cotangent, q_gain, k_gain, frames, heights, widths):
     count = lax.axis_size("dp")
     flat = (SPOTS, CHANNELS)
-    gains = gather_gains(q_gain, k_gain, count)
-    query_grad, key_grad, value_grad, gpart = main_call(
+    results = main_call(
         query_input.reshape(flat),
         key_input.reshape(flat),
         value_input.reshape(flat),
         cotangent.reshape(flat),
-        gains,
+        q_gain,
+        k_gain,
         frames,
         heights,
         widths,
+        count,
     )
-    share_q, share_k = reduce_gains(gpart, count)
+    query_grad, key_grad, value_grad, share_q, share_k = emit(results)
     full = (1, 1, SPOTS, CHANNELS)
     return (
         query_grad.reshape(full),
         key_grad.reshape(full),
         value_grad.reshape(full),
-        share_q,
-        share_k,
+        share_q.reshape(-1),
+        share_k.reshape(-1),
     )
 
 

time: 127 us -> 85.2 us (0.67)
  Pallas kernels: 115 us -> 81.5 us
  local copies, waits for them, and re-layouts: 8.78 us -> 0.66 us
    pallas_call x3 -> x2, Pallas kernels: 115 us -> 81.5 us  [the longest x1 80.1 us: main_call(): pl.pallas_call(functools.partial(main_kernel, count, size), out_shape=(gr...]
    unnamed x21 -> x4, local copies, waits for them, and re-layouts: 8.78 us -> 0.66 us
where the time goes in v2:
time: 85.2 us; the launch traced here: 84.7 us
  Pallas kernels  81.5 us (96%)
  between operations  2.6 us (3%)
    pallas_call x1, Pallas kernels, main_call(): pl.pallas_call(functools.partial(main_kernel, count, size), out_shape=(gr...  80.1 us

profile of v2, /device:TPU:1, one launch (start us, length us, event | category | flops | bytes accessed | tf_op | source)
XLA Modules:
  0.0 84.7 jit_solution(16605416427509353531)
XLA Ops:
  2.6 0.0 copy-start
  2.6 0.0 copy-start.1
  2.6 0.6 copy-done
  3.2 0.0 copy-done.1
  3.2 80.1 %axial.1 = (bf16[240,1536]{1,0:T(8,128)(2,1)S(1)}, bf16[240,1536]{1,0:T(8,128)(2,1)S(1)}, bf16[240,1536]{1,0:T(8,128)(2,1)S(1)}, f32[1,48]{1,0:T(1,128)S(1)}, f32[1,48]{1,0:T(1,128)S(1)}) custom-call(bf16[240,1536]{1,0:T(8,128)(2,1)} %bitcast.13, bf16[240,1536]{1,0:T(8,128)(2,1)} %bitcast.14, bf16[240,1536]{1,0:T(8,128)(2,1)} %bitcast.15, ...), custom_call_target="tpu_custom_call" | custom-call | tf_op jit(solution)/shard_map/axial/pallas_call | solution.py:383
  83.3 1.4 %emit.1 = (bf16[240,1536]{1,0:T(8,128)(2,1)}, bf16[240,1536]{1,0:T(8,128)(2,1)}, bf16[240,1536]{1,0:T(8,128)(2,1)}, f32[1,48]{1,0:T(1,128)}, f32[1,48]{1,0:T(1,128)}) custom-call(bf16[240,1536]{1,0:T(8,128)(2,1)S(1)} %get-tuple-element.15.refs_0_, bf16[240,1536]{1,0:T(8,128)(2,1)S(1)} %get-tuple-element.16.refs_1_, ...), custom_call_target="tpu_custom_call" | custom-call | tf_op jit(solution)/shard_map/emit/pallas_call | solution.py:436
Async XLA Ops:
  2.6 0.7 copy-start
  2.6 0.7 copy-start.1

commit v3 on v2

v3 whole, which is shorter than its diff:
```python
import functools
import math

import jax
import jax.numpy as jnp
from jax import lax
from jax.experimental import pallas as pl
from jax.experimental.pallas import tpu as pltpu
from jax.sharding import PartitionSpec as P

HEADS = 12
DIM = 128
COLS = 16
FRAMES = 16
SPOTS = 240
BLOCK = 16
CHANNELS = HEADS * DIM
AHEAD = 5
AHEAD2 = 2
EARLY = 8
PAIR_S = 2
PAIR_T = 2
DOWN = 0
EPS = 1e-06
NEGATIVE = -1e30
FAR = -2e30
SCALE = 1.0 / math.sqrt(DIM)
LOG2E = math.log2(math.e)
MESH = pl.DeviceIdType.MESH
F32 = jnp.float32
BF16 = jnp.bfloat16


def dot(a, b, dims):
    return lax.dot_general(a, b, (dims, ((), ())), preferred_element_type=F32)


def inverse_norm(values):
    return lax.rsqrt(jnp.sum(values * values, axis=-1, keepdims=True) * (1.0 / DIM) + EPS)


def attend(queries, keys, values, cotan, bias):
    scores = dot(keys, queries, ((1,), (1,))) * (SCALE * LOG2E) + bias
    dprobs = dot(values, cotan, ((1,), (1,)))
    expo = jnp.exp2(scores - jnp.max(scores, axis=0, keepdims=True))
    probs = expo * (1.0 / jnp.sum(expo, axis=0, keepdims=True))
    value_part = dot(probs.astype(BF16), cotan, ((1,), (0,)))
    delta = jnp.sum(probs * dprobs, axis=0, keepdims=True)
    dscores = (probs * (dprobs - delta) * SCALE).astype(BF16)
    key_part = dot(dscores, queries, ((1,), (0,)))
    query_part = dot(dscores, keys, ((0,), (0,)))
    return query_part, key_part, value_part


def partner(me, i):
    if DOWN:
        return 16 - i - jnp.where(16 - i <= me, 1, 0)
    return i - 1 + jnp.where(i > me, 1, 0)


def idle_of(head):
    return jnp.where(head < 11, head, 15)


def piece_of(i, size):
    start = i * size
    return start // DIM, start % DIM, start % DIM + size > DIM


def lead_of(place, count):
    return lax.rem(place + count // 2, count)


def main_kernel(
    count, size,
    q_hbm, k_hbm, v_hbm, c_hbm, q_gain, k_gain, frames, heights, widths,
    dq_hbm, dk_hbm, dv_hbm, share_q, share_k,
    stack, recv, tout, ret, sgrad, outs, bias_t, gains, gpart, piece, spare, pieces, cut, cuts, sums, shares,
    gain_rows, met_sem, small_sem, load_sem, fwd_send, fwd_recv, own_sem, back_send, back_recv, out_sem, gain_sem,
):
    me = lax.axis_index("seq")
    clip = lax.axis_index("dp")

    leads = clip == lead_of(me, count)

    loads = [
        pltpu.make_async_copy(src, stack.at[a], load_sem.at[a])
        for a, src in enumerate((q_hbm, k_hbm, v_hbm, c_hbm))
    ]
    smalls = [
        pltpu.make_async_copy(src, dst, small_sem.at[a])
        for a, (src, dst) in enumerate(
            ((q_gain, gain_rows.at[0]), (k_gain, gain_rows.at[1]))
        )
    ]
    barrier = pltpu.get_barrier_semaphore()

    def greet(i, carry):
        to = lax.rem(me + i, FRAMES)

        @pl.when(clip != lead_of(to, count))
        def _():
            pl.semaphore_signal(barrier, inc=1, device_id={"seq": to}, device_id_type=MESH)

        return carry

    lax.fori_loop(1, FRAMES, greet, 0)
    for load in loads:
        load.start()
    for small in smalls:
        small.start()

    @pl.when(jnp.logical_not(leads))
    def _():
        pl.semaphore_signal(
            barrier, inc=1, device_id={"dp": lead_of(me, count)}, device_id_type=MESH
        )

    for load in loads:
        load.wait()

    @pl.when(jnp.logical_not(leads))
    def _():
        pl.semaphore_wait(barrier, FRAMES - 1)

    mate = lax.rem(me + FRAMES - 1, FRAMES)

    @pl.when(clip == lead_of(mate, count))
    def _():
        pl.semaphore_signal(met_sem.at[0], inc=1, device_id={"seq": mate}, device_id_type=MESH)

    @pl.when(leads)
    def _():
        pl.semaphore_wait(met_sem.at[0], 1)

    def lanes(head):
        return pl.ds(pl.multiple_of(head * DIM, DIM), DIM)

    def rows(block):
        return pl.ds(pl.multiple_of(block * BLOCK, BLOCK), BLOCK)

    def send_head(head, carry):
        idle = idle_of(head)

        def send_one(i, inner):
            to = partner(me, i)
            block = jnp.where(to < 15, to, head)

            @pl.when(to != idle)
            def _():
                pltpu.make_async_remote_copy(
                    src_ref=stack.at[:, rows(block), lanes(head)],
                    dst_ref=recv.at[head, :, rows(me), :],
                    send_sem=fwd_send.at[head],
                    recv_sem=fwd_recv.at[head],
                    device_id={"seq": to},
                    device_id_type=MESH,
                ).start()

            return inner

        lax.fori_loop(1, 16, send_one, 0)

        @pl.when(me != idle)
        def _():
            block = jnp.where(me < 15, me, head)
            pltpu.make_async_copy(
                stack.at[:, rows(block), lanes(head)],
                recv.at[head, :, rows(me), :],
                own_sem.at[head],
            ).start()

        return carry

    ahead = jnp.where(clip < count // 2, AHEAD, AHEAD2)
    lax.fori_loop(0, ahead, send_head, 0)

    for small in smalls:
        small.wait()
    shift = lax.rem(clip * size, DIM)
    piece[...] = jnp.zeros_like(piece)
    spare[...] = jnp.zeros_like(spare)
    piece[0:1, 0:size] = gain_rows[0]
    spare[0:1, 0:size] = gain_rows[1]
    piece[...] = pltpu.roll(piece[...] + pltpu.roll(spare[...], DIM // 2, 1), shift, 1)
    pieces[clip, 0:1] = piece[0:1]

    @pl.when(leads)
    def _():
        pl.semaphore_wait(barrier, count - 1)

        def tell(i, carry):
            to = lax.rem(clip + i, count)
            pl.semaphore_signal(met_sem.at[1], inc=1, device_id={"dp": to}, device_id_type=MESH)
            return carry

        lax.fori_loop(1, count, tell, 0)

    @pl.when(jnp.logical_not(leads))
    def _():
        pl.semaphore_wait(met_sem.at[1], 1)

    def send_piece(i, carry):
        pltpu.make_async_remote_copy(
            src_ref=piece.at[pl.ds(0, 1)],
            dst_ref=pieces.at[clip, pl.ds(0, 1)],
            send_sem=gain_sem.at[0],
            recv_sem=gain_sem.at[1],
            device_id={"dp": lax.rem(clip + i, count)},
            device_id_type=MESH,
        ).start()
        return carry

    lax.fori_loop(1, count, send_piece, 0)
    lax.fori_loop(ahead, HEADS, send_head, 0)

    others = pieces.at[pl.ds(0, count - 1), pl.ds(0, 1)]
    pltpu.make_async_copy(others, others, gain_sem.at[1]).wait()
    lane = lax.broadcasted_iota(jnp.int32, (1, DIM), 1)
    total = [jnp.zeros((1, DIM), F32) for _ in range(2 * HEADS)]
    for i in range(count):
        at, off, spills = piece_of(i, size)
        row = pieces[i, 0:1]
        for a in range(2):
            if a:
                row = pltpu.roll(row, DIM // 2, 1)
            total[at + a * HEADS] += jnp.where((lane >= off) & (lane < off + size), row, 0.0)
            if spills:
                total[at + 1 + a * HEADS] += jnp.where(lane < off + size - DIM, row, 0.0)
    for at in range(2 * HEADS):
        gains[at : at + 1, :] = total[at]

    count_f, count_h, count_w = frames[0], heights[0], widths[0]

    def spot_fits(spot):
        return (spot // COLS < count_h) & (spot % COLS < count_w)

    spot = lax.broadcasted_iota(jnp.int32, (SPOTS, 1), 0)
    valid_s = spot_fits(spot) & (me < count_f)
    bias_s = jnp.where(valid_s, 0.0, NEGATIVE).astype(F32)
    cot_s = jnp.where(valid_s, 1.0, 0.0).astype(BF16)

    def spatial_head(head):
        q32 = stack[0, :, lanes(head)].astype(F32)
        k32 = stack[1, :, lanes(head)].astype(F32)
        gain_q, gain_k = gains[pl.ds(head, 1), :], gains[pl.ds(head + HEADS, 1), :]
        scaled_q, scaled_k = q32 * inverse_norm(q32), k32 * inverse_norm(k32)
        normed_q = (scaled_q * gain_q).astype(BF16)
        normed_k = (scaled_k * gain_k).astype(BF16)
        cotan = stack[3, :, lanes(head)] * cot_s
        part_q, part_k, part_v = attend(normed_q, normed_k, stack[2, :, lanes(head)], cotan, bias_s)
        sgrad[head, 0] = part_q
        sgrad[head, 1] = part_k
        sgrad[head, 2] = part_v
        gpart[pl.ds(head, 1), :] = jnp.sum(part_q * scaled_q, axis=0, keepdims=True)
        gpart[pl.ds(head + HEADS, 1), :] = jnp.sum(part_k * scaled_k, axis=0, keepdims=True)

    def spatial(step, carry):
        for j in range(PAIR_S):
            spatial_head(step * PAIR_S + j)
        return carry

    lax.fori_loop(0, HEADS // PAIR_S, spatial, 0)

    line = lax.broadcasted_iota(jnp.int32, (256, 1), 0)
    key_at = lax.broadcasted_iota(jnp.int32, (256, 256), 0)
    query_at = lax.broadcasted_iota(jnp.int32, (256, 256), 1)
    bias_t[...] = jnp.where(key_at % BLOCK == query_at % BLOCK, 0.0, FAR).astype(F32)

    units = jnp.where((me >= 11) & (me < 15), 12, 11)

    def head_of(unit):
        return unit + jnp.where((me < 11) & (unit >= me), 1, 0)

    def send_back(unit, carry):
        head = head_of(unit)
        block = jnp.where(me < 15, me, head)

        def send_one(i, inner):
            to = partner(me, i)
            pltpu.make_async_remote_copy(
                src_ref=tout.at[head, :, rows(to), :],
                dst_ref=ret.at[head, :, rows(block), :],
                send_sem=back_send.at[head],
                recv_sem=back_recv.at[head],
                device_id={"seq": to},
                device_id_type=MESH,
            ).start()
            return inner

        lax.fori_loop(1, 16, send_one, 0)
        pltpu.make_async_copy(
            tout.at[head, :, rows(me), :], ret.at[head, :, rows(block), :], own_sem.at[head]
        ).start()
        return carry

    def arrive(head):
        whole, own = recv.at[head, :, pl.ds(0, 240), :], recv.at[head, :, pl.ds(0, 16), :]
        pltpu.make_async_copy(whole, whole, fwd_recv.at[head]).wait()
        pltpu.make_async_copy(own, own, own_sem.at[head]).wait()

    def temporal_head(head):
        block = jnp.where(me < 15, me, head)
        valid_t = spot_fits(block * BLOCK + line % BLOCK) & (line // BLOCK < count_f)
        bias = bias_t[...] + jnp.where(valid_t, 0.0, NEGATIVE).astype(F32)
        q32 = recv[head, 0].astype(F32)
        k32 = recv[head, 1].astype(F32)
        gain_q, gain_k = gains[pl.ds(head, 1), :], gains[pl.ds(head + HEADS, 1), :]
        scaled_q, scaled_k = q32 * inverse_norm(q32), k32 * inverse_norm(k32)
        normed_q = (scaled_q * gain_q).astype(BF16)
        normed_k = (scaled_k * gain_k).astype(BF16)
        cotan = recv[head, 3] * jnp.where(valid_t, 1.0, 0.0).astype(BF16)
        part_q, part_k, part_v = attend(normed_q, normed_k, recv[head, 2], cotan, bias)
        part_q, part_k = part_q.astype(BF16), part_k.astype(BF16)
        tout[head, 0] = part_q
        tout[head, 1] = part_k
        tout[head, 2] = part_v.astype(BF16)
        gpart[pl.ds(head, 1), :] += jnp.sum(part_q.astype(F32) * scaled_q, axis=0, keepdims=True)
        gpart[pl.ds(head + HEADS, 1), :] += jnp.sum(
            part_k.astype(F32) * scaled_k, axis=0, keepdims=True
        )

    def temporal(step, carry):
        heads = [head_of(step * PAIR_T + j) for j in range(PAIR_T)]
        for head in heads:
            arrive(head)
        for head in heads:
            temporal_head(head)
        return carry

    def temporal_and_back(unit, carry):
        arrive(head_of(unit))
        temporal_head(head_of(unit))
        return send_back(unit, carry)

    lax.fori_loop(0, EARLY, temporal_and_back, 0)
    lax.fori_loop(EARLY // PAIR_T, 10 // PAIR_T, temporal, 0)
    arrive(head_of(10))
    temporal_head(head_of(10))

    @pl.when((me >= 11) & (me < 15))
    def _():
        arrive(11)
        temporal_head(11)

    for i in range(count):
        at, off, spills = piece_of(i, size)
        parts = []
        for a in range(2):
            row = gpart[at + a * HEADS : at + a * HEADS + 1, :]
            if spills:
                row = jnp.where(lane >= off, row, gpart[at + a * HEADS + 1 : at + a * HEADS + 2, :])
            parts.append(row)
        inside = (lane >= off) & (lane < off + size) | (lane < off + size - DIM)
        cut[i, 0:1, :] = jnp.where(inside, parts[0], pltpu.roll(parts[1], DIM // 2, 1))
    cuts[clip, 0:1] = cut[clip, 0:1]

    def send_cut(i, carry):
        to = lax.rem(clip + i, count)
        pltpu.make_async_remote_copy(
            src_ref=cut.at[to, pl.ds(0, 1)],
            dst_ref=cuts.at[clip, pl.ds(0, 1)],
            send_sem=gain_sem.at[2],
            recv_sem=gain_sem.at[3],
            device_id={"dp": to},
            device_id_type=MESH,
        ).start()
        return carry

    lax.fori_loop(1, count, send_cut, 0)
    lax.fori_loop(EARLY, units, send_back, 0)

    def finish(head, carry):
        idle = idle_of(head)

        @pl.when(me != idle)
        def _():
            pltpu.make_async_copy(
                ret.at[head, :, pl.ds(0, 224), :], ret.at[head, :, pl.ds(0, 224), :], back_recv.at[head]
            ).wait()
            pltpu.make_async_copy(
                ret.at[head, :, pl.ds(0, 16), :], ret.at[head, :, pl.ds(0, 16), :], own_sem.at[head]
            ).wait()

        @pl.when(me == idle)
        def _():
            pltpu.make_async_copy(ret.at[head], ret.at[head], back_recv.at[head]).wait()

        for a in range(2):
            raw = stack[a, :, lanes(head)].astype(F32)
            inverse = inverse_norm(raw)
            gain = gains[pl.ds(head + HEADS * a, 1), :]
            scaled = gain * (sgrad[head, a] + ret[head, a].astype(F32))
            mean = jnp.sum(scaled * raw, axis=-1, keepdims=True) * (1.0 / DIM)
            outs[a, :, lanes(head)] = (
                inverse * scaled - raw * (inverse * inverse * inverse) * mean
            ).astype(BF16)
        outs[2, :, lanes(head)] = (sgrad[head, 2] + ret[head, 2].astype(F32)).astype(BF16)
        for a, dst in enumerate((dq_hbm, dk_hbm, dv_hbm)):
            pltpu.make_async_copy(
                outs.at[a, :, lanes(head)], dst.at[:, lanes(head)], out_sem.at[a]
            ).start()
        return carry

    others = cuts.at[pl.ds(0, count - 1), pl.ds(0, 1)]
    pltpu.make_async_copy(others, others, gain_sem.at[3]).wait()
    summed = jnp.broadcast_to(jnp.sum(cuts[:, 0:1], axis=0), (8, DIM))
    sums[...] = pltpu.roll(summed, lax.rem(DIM - shift, DIM), 1)
    shares[me, 0:1] = sums[0:1]

    def send_sums(i, carry):
        pltpu.make_async_remote_copy(
            src_ref=sums.at[pl.ds(0, 1)],
            dst_ref=shares.at[me, pl.ds(0, 1)],
            send_sem=gain_sem.at[4],
            recv_sem=gain_sem.at[5],
            device_id={"seq": lax.rem(me + i, FRAMES)},
            device_id_type=MESH,
        ).start()
        return carry

    lax.fori_loop(1, FRAMES, send_sums, 0)

    lax.fori_loop(0, HEADS, finish, 0)

    others = shares.at[pl.ds(0, FRAMES - 1), pl.ds(0, 1)]
    pltpu.make_async_copy(others, others, gain_sem.at[5]).wait()
    summed = jnp.sum(shares[:, 0:1], axis=0)
    share_q[...] = summed[:, 0:size]
    share_k[...] = pltpu.roll(summed, DIM // 2, 1)[:, 0:size]

    def drain(head, carry):
        idle = idle_of(head)

        @pl.when(me != idle)
        def _():
            pltpu.make_async_copy(
                recv.at[head, :, pl.ds(0, 224), :], recv.at[head, :, pl.ds(0, 224), :], fwd_send.at[head]
            ).wait()
            pltpu.make_async_copy(
                tout.at[head, :, pl.ds(0, 240), :], tout.at[head, :, pl.ds(0, 240), :], back_send.at[head]
            ).wait()

        @pl.when(me == idle)
        def _():
            pltpu.make_async_copy(
                recv.at[head, :, pl.ds(0, 240), :], recv.at[head, :, pl.ds(0, 240), :], fwd_send.at[head]
            ).wait()

        return carry

    lax.fori_loop(0, HEADS, drain, 0)
    others = cuts.at[pl.ds(0, count - 1), pl.ds(0, 1)]
    pltpu.make_async_copy(others, others, gain_sem.at[0]).wait()
    pltpu.make_async_copy(others, others, gain_sem.at[2]).wait()
    others = shares.at[pl.ds(0, FRAMES - 1), pl.ds(0, 1)]
    pltpu.make_async_copy(others, others, gain_sem.at[4]).wait()
    for a, dst in enumerate((dq_hbm, dk_hbm, dv_hbm)):
        pltpu.make_async_copy(outs.at[a], dst, out_sem.at[a]).wait()


def main_call(q, k, v, c, q_gain, k_gain, frames, heights, widths, count):
    size = q_gain.shape[0]
    any_spec = pl.BlockSpec(memory_space=pl.ANY)
    vmem = pl.BlockSpec(memory_space=pltpu.VMEM)
    smem = pl.BlockSpec(memory_space=pltpu.SMEM)
    grad = jax.ShapeDtypeStruct((SPOTS, CHANNELS), BF16)
    share = jax.ShapeDtypeStruct((1, size), F32)
    arrays = (q, k, v, c, q_gain.reshape(1, size), k_gain.reshape(1, size))
    arrays = [pltpu.with_memory_space_constraint(x, pltpu.HBM) for x in arrays]
    arrays += [frames, heights, widths]
    return pl.pallas_call(
        functools.partial(main_kernel, count, size),
        out_shape=(grad, grad, grad, share, share),
        in_specs=[any_spec] * 6 + [smem] * 3,
        out_specs=(any_spec, any_spec, any_spec, vmem, vmem),
        scratch_shapes=[
            pltpu.VMEM((4, SPOTS, CHANNELS), BF16),
            pltpu.VMEM((HEADS, 4, 256, DIM), BF16),
            pltpu.VMEM((HEADS, 3, 256, DIM), BF16),
            pltpu.VMEM((HEADS, 3, SPOTS, DIM), BF16),
            pltpu.VMEM((HEADS, 3, SPOTS, DIM), F32),
            pltpu.VMEM((3, SPOTS, CHANNELS), BF16),
            pltpu.VMEM((256, 256), F32),
            pltpu.VMEM((2 * HEADS, DIM), F32),
            pltpu.VMEM((2 * HEADS, DIM), F32),
            pltpu.VMEM((8, DIM), F32),
            pltpu.VMEM((8, DIM), F32),
            pltpu.VMEM((count, 8, DIM), F32),
            pltpu.VMEM((count, 8, DIM), F32),
            pltpu.VMEM((count, 8, DIM), F32),
            pltpu.VMEM((8, DIM), F32),
            pltpu.VMEM((FRAMES, 8, DIM), F32),
            pltpu.VMEM((2, 1, size), F32),
            pltpu.SemaphoreType.REGULAR((2,)),
            pltpu.SemaphoreType.DMA((2,)),
            pltpu.SemaphoreType.DMA((4,)),
            pltpu.SemaphoreType.DMA((HEADS,)),
            pltpu.SemaphoreType.DMA((HEADS,)),
            pltpu.SemaphoreType.DMA((HEADS,)),
            pltpu.SemaphoreType.DMA((HEADS,)),
            pltpu.SemaphoreType.DMA((HEADS,)),
            pltpu.SemaphoreType.DMA((3,)),
            pltpu.SemaphoreType.DMA((6,)),
        ],
        compiler_params=pltpu.CompilerParams(
            collective_id=1, has_side_effects=True, vmem_limit_bytes=40 << 20
        ),
        name="axial",
    )(*arrays)


def emit_kernel(*refs):
    half = len(refs) // 2
    sem = refs[-1]
    copies = [
        pltpu.make_async_copy(src, dst, sem.at[i])
        for i, (src, dst) in enumerate(zip(refs[:half], refs[half:-1]))
    ]
    for copy in copies:
        copy.start()
    for copy in copies:
        copy.wait()


def emit(arrays):
    any_spec = pl.BlockSpec(memory_space=pl.ANY)
    vmem = pl.BlockSpec(memory_space=pltpu.VMEM)
    return pl.pallas_call(
        emit_kernel,
        out_shape=tuple(jax.ShapeDtypeStruct(x.shape, x.dtype) for x in arrays),
        in_specs=[vmem] * len(arrays),
        out_specs=(any_spec,) * len(arrays),
        scratch_shapes=[pltpu.SemaphoreType.DMA((len(arrays),))],
        compiler_params=pltpu.CompilerParams(vmem_limit_bytes=8 << 20),
        name="emit",
    )(*arrays)


def shards(query_input, key_input, value_input, cotangent, q_gain, k_gain, frames, heights, widths):
    count = lax.axis_size("dp")
    flat = (SPOTS, CHANNELS)
    results = main_call(
        query_input.reshape(flat),
        key_input.reshape(flat),
        value_input.reshape(flat),
        cotangent.reshape(flat),
        q_gain,
        k_gain,
        frames,
        heights,
        widths,
        count,
    )
    query_grad, key_grad, value_grad, share_q, share_k = emit(results)
    full = (1, 1, SPOTS, CHANNELS)
    return (
        query_grad.reshape(full),
        key_grad.reshape(full),
        value_grad.reshape(full),
        share_q.reshape(-1),
        share_k.reshape(-1),
    )


def solution(mesh):
    tokens = P("dp", "seq", None, None)
    return jax.shard_map(
        shards,
        mesh=mesh,
        in_specs=(tokens,) * 4 + (P("dp"),) * 5,
        out_specs=(tokens,) * 3 + (P("dp"),) * 2,
        check_vma=False,
    )
```

time: 85.2 us -> 80 us (0.939)
  Pallas kernels: 81.5 us -> 77.2 us
    pallas_call x1, Pallas kernels: 80.1 us -> 75.8 us  [main_call(): pl.pallas_call(functools.partial(main_kernel, count, size), out_shape=(gr...]
where the time goes in v3:
time: 80 us; the launch traced here: 79.8 us
  Pallas kernels  77.2 us (96%)
  between operations  2.58 us (3%)
    pallas_call x1, Pallas kernels, main_call(): pl.pallas_call(functools.partial(main_kernel, count, size), out_shape=(gr...  75.8 us

profile of v3, /device:TPU:1, one launch (start us, length us, event | category | flops | bytes accessed | tf_op | source)
XLA Modules:
  0.0 79.8 jit_solution(5369545264074599507)
XLA Ops:
  2.6 75.8 %axial.1 = (bf16[240,1536]{1,0:T(8,128)(2,1)S(1)}, bf16[240,1536]{1,0:T(8,128)(2,1)S(1)}, bf16[240,1536]{1,0:T(8,128)(2,1)S(1)}, f32[1,48]{1,0:T(1,128)S(1)}, f32[1,48]{1,0:T(1,128)S(1)}) custom-call(bf16[240,1536]{1,0:T(8,128)(2,1)} %bitcast.11, bf16[240,1536]{1,0:T(8,128)(2,1)} %bitcast.12, bf16[240,1536]{1,0:T(8,128)(2,1)} %bitcast.13, ...), custom_call_target="tpu_custom_call" | custom-call | tf_op jit(solution)/shard_map/axial/pallas_call | solution.py:472
  78.4 1.4 %emit.1 = (bf16[240,1536]{1,0:T(8,128)(2,1)}, bf16[240,1536]{1,0:T(8,128)(2,1)}, bf16[240,1536]{1,0:T(8,128)(2,1)}, f32[1,48]{1,0:T(1,128)}, f32[1,48]{1,0:T(1,128)}) custom-call(bf16[240,1536]{1,0:T(8,128)(2,1)S(1)} %get-tuple-element.15.refs_0_, bf16[240,1536]{1,0:T(8,128)(2,1)S(1)} %get-tuple-element.16.refs_1_, ...), custom_call_target="tpu_custom_call" | custom-call | tf_op jit(solution)/shard_map/emit/pallas_call | solution.py:529

commit v4 on v3

--- a/solution.py
+++ b/solution.py
@@ -15,12 +15,13 @@
 SPOTS = 240
 BLOCK = 16
 CHANNELS = HEADS * DIM
-AHEAD = 5
-AHEAD2 = 2
+AHEAD = 8
+AHEAD2 = 4
 EARLY = 8
 PAIR_S = 2
 PAIR_T = 2
-DOWN = 0
+FROM = 12
+FIRST = 6
 EPS = 1e-06
 NEGATIVE = -1e30
 FAR = -2e30
@@ -53,8 +54,6 @@
 
 
 def partner(me, i):
-    if DOWN:
-        return 16 - i - jnp.where(16 - i <= me, 1, 0)
     return i - 1 + jnp.where(i > me, 1, 0)
 
 
@@ -139,37 +138,35 @@
     def rows(block):
         return pl.ds(pl.multiple_of(block * BLOCK, BLOCK), BLOCK)
 
-    def send_head(head, carry):
+    def send_unit(head, to):
         idle = idle_of(head)
-
-        def send_one(i, inner):
-            to = partner(me, i)
-            block = jnp.where(to < 15, to, head)
-
-            @pl.when(to != idle)
-            def _():
-                pltpu.make_async_remote_copy(
-                    src_ref=stack.at[:, rows(block), lanes(head)],
-                    dst_ref=recv.at[head, :, rows(me), :],
-                    send_sem=fwd_send.at[head],
-                    recv_sem=fwd_recv.at[head],
-                    device_id={"seq": to},
-                    device_id_type=MESH,
-                ).start()
-
-            return inner
-
-        lax.fori_loop(1, 16, send_one, 0)
-
-        @pl.when(me != idle)
-        def _():
-            block = jnp.where(me < 15, me, head)
+        block = jnp.where(to < 15, to, head)
+
+        @pl.when((to != idle) & (to != me))
+        def _():
+            pltpu.make_async_remote_copy(
+                src_ref=stack.at[:, rows(block), lanes(head)],
+                dst_ref=recv.at[head, :, rows(me), :],
+                send_sem=fwd_send.at[head],
+                recv_sem=fwd_recv.at[head],
+                device_id={"seq": to},
+                device_id_type=MESH,
+            ).start()
+
+        @pl.when((to != idle) & (to == me))
+        def _():
             pltpu.make_async_copy(
                 stack.at[:, rows(block), lanes(head)],
                 recv.at[head, :, rows(me), :],
                 own_sem.at[head],
             ).start()
 
+    def send_head(head, carry):
+        def one(i, inner):
+            send_unit(head, lax.rem(i + FROM, FRAMES))
+            return inner
+
+        lax.fori_loop(0, FRAMES, one, 0)
         return carry
 
     ahead = jnp.where(clip < count // 2, AHEAD, AHEAD2)
@@ -402,6 +399,8 @@
             ).start()
         return carry
 
+    lax.fori_loop(0, FIRST, finish, 0)
+
     others = cuts.at[pl.ds(0, count - 1), pl.ds(0, 1)]
     pltpu.make_async_copy(others, others, gain_sem.at[3]).wait()
     summed = jnp.broadcast_to(jnp.sum(cuts[:, 0:1], axis=0), (8, DIM))
@@ -421,7 +420,7 @@
 
     lax.fori_loop(1, FRAMES, send_sums, 0)
 
-    lax.fori_loop(0, HEADS, finish, 0)
+    lax.fori_loop(FIRST, HEADS, finish, 0)
 
     others = shares.at[pl.ds(0, FRAMES - 1), pl.ds(0, 1)]
     pltpu.make_async_copy(others, others, gain_sem.at[5]).wait()

time: 80 us -> 77.2 us (0.965)
  Pallas kernels: 77.2 us -> 74.4 us
    pallas_call x1, Pallas kernels: 75.8 us -> 73 us  [main_call(): pl.pallas_call(functools.partial(main_kernel, count, size), out_shape=(gr...]
where the time goes in v4:
time: 77.2 us; the launch traced here: 77 us
  Pallas kernels  74.4 us (96%)
  between operations  2.58 us (3%)
    pallas_call x1, Pallas kernels, main_call(): pl.pallas_call(functools.partial(main_kernel, count, size), out_shape=(gr...  73 us

profile of v4, /device:TPU:1, one launch (start us, length us, event | category | flops | bytes accessed | tf_op | source)
XLA Modules:
  0.0 77.0 jit_solution(13358981361212738258)
XLA Ops:
  2.6 73.0 %axial.1 = (bf16[240,1536]{1,0:T(8,128)(2,1)S(1)}, bf16[240,1536]{1,0:T(8,128)(2,1)S(1)}, bf16[240,1536]{1,0:T(8,128)(2,1)S(1)}, f32[1,48]{1,0:T(1,128)S(1)}, f32[1,48]{1,0:T(1,128)S(1)}) custom-call(bf16[240,1536]{1,0:T(8,128)(2,1)} %bitcast.11, bf16[240,1536]{1,0:T(8,128)(2,1)} %bitcast.12, bf16[240,1536]{1,0:T(8,128)(2,1)} %bitcast.13, ...), custom_call_target="tpu_custom_call" | custom-call | tf_op jit(solution)/shard_map/axial/pallas_call | solution.py:471
  75.6 1.4 %emit.1 = (bf16[240,1536]{1,0:T(8,128)(2,1)}, bf16[240,1536]{1,0:T(8,128)(2,1)}, bf16[240,1536]{1,0:T(8,128)(2,1)}, f32[1,48]{1,0:T(1,128)}, f32[1,48]{1,0:T(1,128)}) custom-call(bf16[240,1536]{1,0:T(8,128)(2,1)S(1)} %get-tuple-element.15.refs_0_, bf16[240,1536]{1,0:T(8,128)(2,1)S(1)} %get-tuple-element.16.refs_1_, ...), custom_call_target="tpu_custom_call" | custom-call | tf_op jit(solution)/shard_map/emit/pallas_call | solution.py:528

commit v5 on v4

--- a/solution.py
+++ b/solution.py
@@ -15,10 +15,10 @@
 SPOTS = 240
 BLOCK = 16
 CHANNELS = HEADS * DIM
-AHEAD = 8
-AHEAD2 = 4
+AHEAD = 10
+AHEAD2 = 5
 EARLY = 8
-PAIR_S = 2
+PAIR_S = 3
 PAIR_T = 2
 FROM = 12
 FIRST = 6

time: 77.2 us -> 76.9 us (level)
  no operation moved by 1% of the time
where the time goes in v5:
time: 76.9 us; the launch traced here: 76.7 us
  Pallas kernels  74.2 us (96%)
  between operations  2.58 us (3%)
    pallas_call x1, Pallas kernels, main_call(): pl.pallas_call(functools.partial(main_kernel, count, size), out_shape=(gr...  72.8 us

profile of v5, /device:TPU:1, one launch (start us, length us, event | category | flops | bytes accessed | tf_op | source)
XLA Modules:
  0.0 76.7 jit_solution(6470133146892445674)
XLA Ops:
  2.6 72.8 %axial.1 = (bf16[240,1536]{1,0:T(8,128)(2,1)S(1)}, bf16[240,1536]{1,0:T(8,128)(2,1)S(1)}, bf16[240,1536]{1,0:T(8,128)(2,1)S(1)}, f32[1,48]{1,0:T(1,128)S(1)}, f32[1,48]{1,0:T(1,128)S(1)}) custom-call(bf16[240,1536]{1,0:T(8,128)(2,1)} %bitcast.11, bf16[240,1536]{1,0:T(8,128)(2,1)} %bitcast.12, bf16[240,1536]{1,0:T(8,128)(2,1)} %bitcast.13, ...), custom_call_target="tpu_custom_call" | custom-call | tf_op jit(solution)/shard_map/axial/pallas_call | solution.py:471
  75.3 1.4 %emit.1 = (bf16[240,1536]{1,0:T(8,128)(2,1)}, bf16[240,1536]{1,0:T(8,128)(2,1)}, bf16[240,1536]{1,0:T(8,128)(2,1)}, f32[1,48]{1,0:T(1,128)}, f32[1,48]{1,0:T(1,128)}) custom-call(bf16[240,1536]{1,0:T(8,128)(2,1)S(1)} %get-tuple-element.15.refs_0_, bf16[240,1536]{1,0:T(8,128)(2,1)S(1)} %get-tuple-element.16.refs_1_, ...), custom_call_target="tpu_custom_call" | custom-call | tf_op jit(solution)/shard_map/emit/pallas_call | solution.py:528
